TPU v7x, 128 devices: a whole 4x4x4 slice. The times are simulated.
128 devices in a mesh: band: 8 (over x, y_lo), domain: 16 (over y_hi, z, core).
Axes of the slice: x: 4, y: 4 (y_hi: 2, y_lo: 2; y = y_hi * 2 + y_lo), z: 4, core: 2. Of those that a mesh axis runs over, the one named last changes fastest.
Arguments:
- orbitals: float32 [96, 32, 24, 1024], P('domain', None, None, 'band'), may hold values from -6 to 6
- potential: float32 [96, 32, 24], P('domain'), may hold values from -3 to 0
Outputs:
- filtered: float32 [96, 32, 24, 1024], P('domain', None, None, 'band')
- margin: float32 [1024, 1024], P('band', 'domain')
All inputs are finite; a program needn't handle non-finite values.
Results may differ from a plain program's by a relative error of at most 0.00005.
Values sent between devices are 32-bit elements; how exact they have to be, the bound alone decides.
No kernel may reach another device: no remote copies, remote signals or barrier semaphores. Data moves between devices by JAX's collectives and lax.ppermute only.
A program may use at most 192 MiB of HBM per device.

v0:
```python
import jax
import jax.numpy as jnp
from jax import lax
from jax.sharding import PartitionSpec as P

DEG = 3


coeffs = (
    -5369.0 / 1800.0,
    12.0 / 7.0,
    -15.0 / 56.0,
    10.0 / 189.0,
    -1.0 / 112.0,
    2.0 / 1925.0,
    -1.0 / 16632.0,
)
bound_floor = 0.0
bound_cut = 2.0
bound_top = 11.0


def extended(cells, sides, width):
    for axis, dim in sides:
        count = lax.axis_size(axis)
        head = lax.slice_in_dim(cells, 0, width, axis=dim)
        tail = lax.slice_in_dim(cells, cells.shape[dim] - width, cells.shape[dim], axis=dim)
        cells = jnp.concatenate(
            [
                lax.ppermute(tail, axis, [(i, (i + 1) % count) for i in range(count)]),
                cells,
                lax.ppermute(head, axis, [((i + 1) % count, i) for i in range(count)]),
            ],
            axis=dim,
        )
    return cells


def apply_ham(field, potential):
    padded = extended(field, (("domain", 0),), 6)
    planes = field.shape[0]
    total = 3.0 * coeffs[0] * field
    for step in range(1, 7):
        cycle = padded[6 + step : 6 + step + planes] + padded[6 - step : 6 - step + planes]
        cycle = cycle + jnp.roll(field, step, 1) + jnp.roll(field, -step, 1)
        cycle = cycle + jnp.roll(field, step, 2) + jnp.roll(field, -step, 2)
        total = total + coeffs[step] * cycle
    return -0.5 * total + potential[..., None] * field


def inner_block(left, right):
    return lax.dot_general(
        left,
        right,
        (((0,), (0,)), ((), ())),
        precision=lax.Precision.HIGHEST,
        preferred_element_type=jnp.float32,
    )


def local(orbitals, potential):
    half_width = (bound_top - bound_cut) / 2.0
    center = (bound_top + bound_cut) / 2.0
    sigma = half_width / (bound_floor - center)
    gamma = 2.0 / sigma
    prior = orbitals
    current = (apply_ham(orbitals, potential) - center * orbitals) * (sigma / half_width)
    for index in range(2, DEG + 1):
        second = 1.0 / (gamma - sigma)
        nxt = (apply_ham(current, potential) - center * current) * (
            2.0 * second / half_width
        ) - sigma * second * prior
        prior = current
        current = nxt
        sigma = second
    width = current.shape[-1]
    flat = current.reshape(-1, width)
    cells_all = flat.shape[0] * lax.axis_size("domain")
    row_terms = inner_block(flat, lax.all_gather(flat, "band", axis=1, tiled=True))
    margin = lax.psum_scatter(
        row_terms * (1.0 / cells_all), "domain", scatter_dimension=1, tiled=True
    )
    return (current, margin)


def solution(mesh):
    in_specs = (P("domain", None, None, "band"), P("domain", None, None))
    out_specs = (P("domain", None, None, "band"), P("band", "domain"))
    return jax.shard_map(local, mesh=mesh, in_specs=in_specs, out_specs=out_specs, check_vma=False)
```

profile of v0, /device:TPU:0, one launch (start us, length us, event | category | flops | bytes accessed | tf_op | source)
XLA Modules:
  0.0 723.0 jit_solution(14801683073102709037)
XLA Ops:
  7.3 6.3 collective-permute-start
  13.6 4.9 fusion.196
  51.9 2.5 fusion.208
  54.4 2.5 fusion.212
  57.0 2.6 fusion.216
  61.9 3.6 constant_dynamic-update-slice_fusion
  66.7 27.5 %broadcast_multiply_fusion = (f32[6,32,24,128]{3,2,1,0:T(8,128)S(1)}, f32[6,32,24,128]{3,2,1,0:T(8,128)}) fusion(f32[6,32,24,128]{3,2,1,0:T(8,128)S(1)} %copy-done, f32[6,32,24]{2,1,0:T(8,128)S(1)} %copy-done.10, f32[6,32,6,128]{3,2,1,0:T(8,128)} %get-tuple-element.147, f32[6,32,18,128]{3,2,1,0:T(8,128)} %get-tuple-element.149, ...), kind=kLoop, calls=%fused_computation.189 | loop fusion | flops 43057152 | bytes 92030976 | tf_op jit(solution)/shard_map/mul | solution.py:67
  94.1 2.5 fusion.169
  120.7 2.6 fusion.173
  123.3 2.5 fusion.177
  128.3 2.6 fusion.185
  130.9 2.7 fusion.189
  133.6 11.4 %collective-permute-done.2 = f32[6,32,24,128]{3,2,1,0:T(8,128)S(1)} collective-permute-done((f32[6,32,24,128]{3,2,1,0:T(8,128)S(1)}, f32[6,32,24,128]{3,2,1,0:T(8,128)S(1)}, u32[]{:S(2)}, u32[]{:S(2)}) %collective-permute-start.2) | collective-permute-done | bytes 2359328 | tf_op jit(solution)/shard_map/ppermute | solution.py:32
  145.0 5.5 collective-permute-done.3
  151.9 27.3 %fusion.57 = f32[6,32,24,128]{3,2,1,0:T(8,128)S(1)} fusion(f32[6,32,24,128]{3,2,1,0:T(8,128)} %copy-done.9, f32[6,32,24,128]{3,2,1,0:T(8,128)S(1)} %get-tuple-element.2, f32[6,32,24,128]{3,2,1,0:T(8,128)} %copy-done.8, f32[6,31,24,128]{3,2,1,0:T(8,128)} %get-tuple-element.97, f32[6,1,24,128]{3,2,1,0:T(8,128)} %get-tuple-element.99, ...), kind=kLoop, calls=%fused_computation.89 | loop fusion | flops 50135040 | bytes 70797312 | tf_op jit(solution)/shard_map/sub | solution.py:70
  205.5 2.5 fusion.153
  210.5 2.5 fusion.161
  213.0 2.5 fusion.145
  215.6 2.6 fusion.165
  218.4 5.5 collective-permute-done.5
  225.3 27.1 %fusion.14 = f32[6,32,24,128]{3,2,1,0:T(8,128)} fusion(f32[6,32,24,128]{3,2,1,0:T(8,128)} %copy-done.7, f32[6,32,24,128]{3,2,1,0:T(8,128)S(1)} %fusion.57, f32[6,32,24,128]{3,2,1,0:T(8,128)} %copy-done.6, f32[6,31,24,128]{3,2,1,0:T(8,128)} %get-tuple-element.49, f32[6,1,24,128]{3,2,1,0:T(8,128)} %get-tuple-element.51, ...), kind=kLoop, calls=%fused_computation.46 | loop fusion | flops 50135040 | bytes 68438016 | tf_op jit(solution)/shard_map/sub | solution.py:70
  252.7 363.2 %all-gather.2.cloned.1.call-done = f32[4608,1024]{1,0:T(8,128)} async-done(((f32[4608,128]{1,0:T(8,128)}), f32[4608,1024]{1,0:T(8,128)}) %all-gather.2.cloned.1.call-update) | async-done | bytes 18874384 | tf_op jit(solution)/shard_map/all_gather | solution.py:79
  615.9 32.9 %convolution_multiply_fusion = f32[128,1024]{0,1:T(8,128)} fusion(f32[4608,128]{1,0:T(8,128)S(1)} %bitcast.4, f32[4608,1024]{1,0:T(8,128)} %all-gather.2.cloned.1.call-done), kind=kOutput, calls=%fused_computation.188 | convolution fusion | flops 7247888384 | bytes 21757952 | tf_op jit(solution)/shard_map/dot_general | solution.py:52
  648.8 67.3 %reduce-scatter.2.cloned.1.call-done = f32[128,64]{0,1:T(8,128)} async-done(((f32[128,1024]{0,1:T(8,128)}), f32[128,64]{0,1:T(8,128)}) %reduce-scatter.2.cloned.1.call-update) | async-done | bytes 32784 | tf_op jit(solution)/shard_map/reduce_scatter | solution.py:80
  (100 shorter events, 95.7 us)
Async XLA Ops:
  7.2 11.3 %copy-start = (f32[6,32,24,128]{3,2,1,0:T(8,128)S(1)}, f32[6,32,24,128]{3,2,1,0:T(8,128)}, u32[]{:S(2)}) copy-start(f32[6,32,24,128]{3,2,1,0:T(8,128)} %param.2) | copy-start | bytes 7077892
  7.2 608.7 %all-gather.2.cloned.1.call-start = ((), (), s32[]{:S(2)}) async-start(), calls=%async_computation.1 | async-start | bytes 21233664 | tf_op jit(solution)/shard_map/all_gather | solution.py:79
  7.2 52.3 %collective-permute-start.1 = (f32[6,32,24,128]{3,2,1,0:T(8,128)}, f32[6,32,24,128]{3,2,1,0:T(8,128)}, u32[]{:S(2)}, u32[]{:S(2)}) collective-permute-start(f32[6,32,24,128]{3,2,1,0:T(8,128)} %param.2), channel_id=1, source_target_pairs={{0,1},{1,2},{2,3},{3,4},{4,5},{5,6},{6,7},{7,8},{8,9},{9,10},{10,1... | collective-permute-start | bytes 7077896 | tf_op jit(solution)/shard_map/ppermute | solution.py:30
  7.3 54.5 %collective-permute-start = (f32[6,32,24,128]{3,2,1,0:T(8,128)}, f32[6,32,24,128]{3,2,1,0:T(8,128)}, u32[]{:S(2)}, u32[]{:S(2)}) collective-permute-start(f32[6,32,24,128]{3,2,1,0:T(8,128)} %param.2), channel_id=1, source_target_pairs={{1,0},{2,1},{3,2},{4,3},{5,4},{6,5},{7,6},{8,7},{9,8},{10,9},{11,1... | collective-permute-start | bytes 7077896 | tf_op jit(solution)/shard_map/ppermute | solution.py:32
  36.5 4.8 copy-start.11
  61.3 4.1 copy-start.10
  61.8 3.6 copy-start.1
  61.9 4.1 copy-start.4
  61.9 4.8 copy-start.5
  118.0 27.0 %collective-permute-start.2 = (f32[6,32,24,128]{3,2,1,0:T(8,128)S(1)}, f32[6,32,24,128]{3,2,1,0:T(8,128)S(1)}, u32[]{:S(2)}, u32[]{:S(2)}) collective-permute-start(f32[6,32,24,128]{3,2,1,0:T(8,128)S(1)} %get-tuple-element.2), channel_id=1, source_target_pairs={{1,0},{2,1},{3,2},{4,3},{5,4},{6,5},{7,6},{8,7},{9,8},{10,9},{11,1... | collective-permute-start | bytes 7077896 | tf_op jit(solution)/shard_map/ppermute | solution.py:32
  118.6 31.9 %collective-permute-start.3 = (f32[6,32,24,128]{3,2,1,0:T(8,128)S(1)}, f32[6,32,24,128]{3,2,1,0:T(8,128)S(1)}, u32[]{:S(2)}, u32[]{:S(2)}) collective-permute-start(f32[6,32,24,128]{3,2,1,0:T(8,128)S(1)} %get-tuple-element.2), channel_id=1, source_target_pairs={{0,1},{1,2},{2,3},{3,4},{4,5},{5,6},{6,7},{7,8},{8,9},{9,10},{10,1... | collective-permute-start | bytes 7077896 | tf_op jit(solution)/shard_map/ppermute | solution.py:30
  145.0 5.5 copy-start.8
  150.5 1.4 copy-start.9
  191.2 27.1 %collective-permute-start.4 = (f32[6,32,24,128]{3,2,1,0:T(8,128)S(1)}, f32[6,32,24,128]{3,2,1,0:T(8,128)S(1)}, u32[]{:S(2)}, u32[]{:S(2)}) collective-permute-start(f32[6,32,24,128]{3,2,1,0:T(8,128)S(1)} %fusion.57), channel_id=1, source_target_pairs={{1,0},{2,1},{3,2},{4,3},{5,4},{6,5},{7,6},{8,7},{9,8},{10,9},{11,1... | collective-permute-start | bytes 7077896 | tf_op jit(solution)/shard_map/ppermute | solution.py:32
  192.0 31.9 %collective-permute-start.5 = (f32[6,32,24,128]{3,2,1,0:T(8,128)S(1)}, f32[6,32,24,128]{3,2,1,0:T(8,128)S(1)}, u32[]{:S(2)}, u32[]{:S(2)}) collective-permute-start(f32[6,32,24,128]{3,2,1,0:T(8,128)S(1)} %fusion.57), channel_id=1, source_target_pairs={{0,1},{1,2},{2,3},{3,4},{4,5},{5,6},{6,7},{7,8},{8,9},{9,10},{10,1... | collective-permute-start | bytes 7077896 | tf_op jit(solution)/shard_map/ppermute | solution.py:30
  215.6 9.7 %copy-start.2 = (f32[6,32,24,128]{3,2,1,0:T(8,128)S(1)}, f32[6,32,24,128]{3,2,1,0:T(8,128)}, u32[]{:S(2)}) copy-start(f32[6,32,24,128]{3,2,1,0:T(8,128)} %get-tuple-element.3) | copy-start | bytes 7077892
  218.4 5.5 copy-start.6
  223.9 1.4 copy-start.7
  252.3 363.6 %copy-start.3 = (f32[6,32,24,128]{3,2,1,0:T(8,128)S(1)}, f32[6,32,24,128]{3,2,1,0:T(8,128)}, u32[]{:S(2)}) copy-start(f32[6,32,24,128]{3,2,1,0:T(8,128)} %fusion.14) | copy-start | bytes 7077892
  252.4 463.8 %reduce-scatter.2.cloned.1.call-start = ((), (), s32[]{:S(2)}) async-start(), calls=%async_computation.2 | async-start | bytes 557056 | tf_op jit(solution)/shard_map/reduce_scatter | solution.py:80
Sparse Core Ops, SparseCore 0:
  252.5 363.3 all-gather.1
  649.0 67.1 reduce-scatter.1
where the time goes:
time: 723 us
  waiting for transfers between devices  453 us (63%)
  local copies, waits for them, and re-layouts  132 us (18%)
  other arithmetic  82.5 us (11%)
  matrix products  32.9 us (5%)
  between operations  14.2 us (2%)
  starting transfers between devices  8.13 us (1%)
    all_gather x1, waiting for transfers between devices, local(): lax.all_gather(flat, 'band', axis=1, tiled=True)  363 us
    reduce_scatter x1, waiting for transfers between devices, local(): lax.psum_scatter(row_terms * (1.0 / cells_all), 'domain', scatter_dimensi...  67.3 us
    slice x36, local copies, waits for them, and re-layouts, apply_ham(): cycle = cycle + jnp.roll(field, step, 2) + jnp.roll(field, -step, 2)  63.4 us
    slice x36, local copies, waits for them, and re-layouts, apply_ham(): cycle = cycle + jnp.roll(field, step, 1) + jnp.roll(field, -step, 1)  55.6 us
    sub x2, other arithmetic, local(): (apply_ham(current, potential) - center * current) * (2.0 * second / half...  54.4 us
    dot_general x1, matrix products, inner_block(): lax.dot_general(left, right, (((0,), (0,)), ((), ())), precision=lax.Prec...  32.9 us
    mul x1, other arithmetic, local(): (apply_ham(orbitals, potential) - center * orbitals) * (sigma / half_width)  27.5 us
  transfers between devices with their start and end apart: 8, of which 6 were waited for; matrix products, arithmetic and copies ran while one was open for 12% of the time, Pallas kernels for 0%

commit v1 on v0

v1 whole, which is shorter than its diff:
```python
import jax
import jax.numpy as jnp
import numpy as np
from jax import lax
from jax.experimental import pallas as pl
from jax.experimental.pallas import tpu as pltpu
from jax.sharding import PartitionSpec as P

DEG = 3

coeffs = (
    -5369.0 / 1800.0,
    12.0 / 7.0,
    -15.0 / 56.0,
    10.0 / 189.0,
    -1.0 / 112.0,
    2.0 / 1925.0,
    -1.0 / 16632.0,
)
bound_floor = 0.0
bound_cut = 2.0
bound_top = 11.0
center = (bound_top + bound_cut) / 2.0

NX, NY, NZ = 96, 32, 24
PTS = NY * NZ
LT = PTS // 128
BANDS, DOMS = 8, 16
PL = NX // DOMS
NORB = 1024
OB = NORB // BANDS
OD = OB // DOMS
ROWS = PL * LT * OD
POT = PL * LT
POT_PAD = 40
GRID = NX * PTS
VMEM = 60 * 1024 * 1024


def steps():
    half_width = (bound_top - bound_cut) / 2.0
    sigma = half_width / (bound_floor - center)
    gamma = 2.0 / sigma
    out = [(sigma / half_width, 0.0)]
    for _ in range(2, DEG + 1):
        second = 1.0 / (gamma - sigma)
        out.append((2.0 * second / half_width, sigma * second))
        sigma = second
    return out


def plane_matrix():
    def ring(n):
        m = np.zeros((n, n))
        for k in range(1, 7):
            for i in range(n):
                m[i, (i + k) % n] += coeffs[k]
                m[i, (i - k) % n] += coeffs[k]
        return m

    m = np.kron(ring(NY), np.eye(NZ)) + np.kron(np.eye(NY), ring(NZ))
    m = -0.5 * (m + 3.0 * coeffs[0] * np.eye(PTS))
    hi = np.asarray(m, jnp.bfloat16)
    lo = np.asarray(m - hi.astype(np.float64), jnp.bfloat16)
    return hi, lo


def split(value):
    hi = value.astype(jnp.bfloat16)
    return hi, (value - hi.astype(jnp.float32)).astype(jnp.bfloat16)


def spread_kernel(cells, pot, out):
    for p in range(PL):
        flat = cells[p].T
        for j in range(LT):
            at = (p * LT + j) * OD
            out[:, at : at + OD, :] = flat[:, j * 128 : (j + 1) * 128].reshape(DOMS, OD, 128)
    row = jnp.concatenate([pot[...], jnp.zeros((POT_PAD - POT, 128), jnp.float32)], 0)
    out[:, ROWS:, :] = jnp.broadcast_to(row[None], (DOMS, POT_PAD, 128))


def filter_kernel(cells, high, low, out, other, left, prod):
    def keep(s, j, i, pair):
        value = jnp.concatenate(pair, 0)
        hi, lo = split(value)
        at = pl.ds(pl.multiple_of(s * (PL * OD), 16) + (i - 1) * OD, 2 * OD)
        left[at, j * 128 : (j + 1) * 128] = hi
        left[at, PTS + j * 128 : PTS + (j + 1) * 128] = lo

    @pl.loop(0, DOMS)
    def _(s):
        for j in range(LT):
            tiles = [cells[s, (i * LT + j) * OD : (i * LT + j + 1) * OD, :] for i in range(PL)]
            for i in range(1, PL, 2):
                keep(s, j, i, tiles[i - 1 : i + 1])

    def step(cur, prior, new, scale, back, last):
        for n in range(PTS // 256):
            cols = slice(n * 256, (n + 1) * 256)
            prod[:, cols] = (
                jnp.dot(left[:, :PTS], high[:, cols], preferred_element_type=jnp.float32)
                + jnp.dot(left[:, PTS:], high[:, cols], preferred_element_type=jnp.float32)
                + jnp.dot(left[:, :PTS], low[:, cols], preferred_element_type=jnp.float32)
            )

        @pl.loop(0, DOMS)
        def _(s):
            before = lax.rem(s + DOMS - 1, DOMS)
            after = lax.rem(s + 1, DOMS)
            for j in range(LT):
                at = [slice((i * LT + j) * OD, (i * LT + j + 1) * OD) for i in range(PL)]
                line = [cur[b, at[i], :] for b in (before, s, after) for i in range(PL)]
                fresh = []
                for i in range(PL):
                    mid = PL + i
                    pot = cells[s, ROWS + i * LT + j, :][None]
                    rows = pl.ds(pl.multiple_of(s * (PL * OD), 16) + i * OD, OD)
                    total = prod[rows, j * 128 : (j + 1) * 128] + (pot - center) * line[mid]
                    for k in range(1, 7):
                        total = total + (-0.5 * coeffs[k]) * (line[mid + k] + line[mid - k])
                    value = scale * total
                    if prior is not None:
                        value = value - back * prior[s, at[i], :]
                    fresh.append(value)
                for i in range(PL):
                    new[s, at[i], :] = fresh[i]
                    if not last and i % 2:
                        keep(s, j, i, fresh[i - 1 : i + 1])

    (a0, _), (a1, b1), (a2, b2) = steps()
    step(cells, None, other, a0, 0.0, False)
    step(other, cells, out, a1, b1, False)
    step(out, other, other, a2, b2, True)
    out[...] = other[...]


def gather_kernel(cells, out):
    for p in range(PL):
        for j in range(LT):
            at = (p * LT + j) * OD
            tile = cells[:, at : at + OD, :].reshape(OB, 128)
            out[p * PTS + j * 128 : p * PTS + (j + 1) * 128, :] = tile.T


def margin_kernel(cells, out):
    his, los = [], []
    for b in range(BANDS):
        hi, lo = split(cells[b])
        his.append(hi)
        los.append(lo)
    hi, lo = jnp.concatenate(his, 1), jnp.concatenate(los, 1)

    def dot(x, y):
        return lax.dot_general(x, y, (((0,), (0,)), ((), ())), preferred_element_type=jnp.float32)

    for b in range(0, BANDS, 2):
        cols = slice(b * OB, (b + 2) * OB)
        block = dot(hi, hi[:, cols]) + dot(lo, hi[:, cols]) + dot(hi, lo[:, cols])
        out[b] = block[:, :OB].reshape(DOMS, NORB // DOMS, OB)
        out[b + 1] = block[:, OB:].reshape(DOMS, NORB // DOMS, OB)


def sum_kernel(parts, out):
    total = parts[0]
    for i in range(1, BANDS * DOMS):
        total = total + parts[i]
    out[...] = (total * (1.0 / GRID)).T


def call(kernel, shape, *args, scratch=()):
    return pl.pallas_call(
        kernel,
        out_shape=jax.ShapeDtypeStruct(shape, jnp.float32),
        scratch_shapes=list(scratch),
        compiler_params=pltpu.CompilerParams(vmem_limit_bytes=VMEM),
    )(*args)


def local(orbitals, potential, high, low):
    cells = call(
        spread_kernel,
        (DOMS, ROWS + POT_PAD, 128),
        orbitals.reshape(PL, PTS, OB),
        potential.reshape(POT, 128),
    )
    cells = lax.all_to_all(cells, "domain", 0, 0, tiled=True)
    cells = call(
        filter_kernel,
        (DOMS, ROWS, 128),
        cells,
        high,
        low,
        scratch=[
            pltpu.VMEM((DOMS, ROWS, 128), jnp.float32),
            pltpu.VMEM((NX * OD, 2 * PTS), jnp.bfloat16),
            pltpu.VMEM((NX * OD, PTS), jnp.float32),
        ],
    )
    cells = lax.all_to_all(cells, "domain", 0, 0, tiled=True)
    flat = call(gather_kernel, (PL * PTS, OB), cells)
    points = lax.all_to_all(flat.reshape(BANDS, PL * PTS // BANDS, OB), "band", 0, 0, tiled=True)
    partial = call(margin_kernel, (BANDS, DOMS, NORB // DOMS, OB), points)
    partial = partial.reshape(BANDS * DOMS, NORB // DOMS, OB)
    partial = lax.all_to_all(partial, ("band", "domain"), 0, 0, tiled=True)
    margin = call(sum_kernel, (OB, NORB // DOMS), partial)
    return flat.reshape(PL, NY, NZ, OB), margin


def solution(mesh):
    grid, pot = P("domain", None, None, "band"), P("domain", None, None)
    high, low = plane_matrix()
    body = jax.shard_map(
        local,
        mesh=mesh,
        in_specs=(grid, pot, P(), P()),
        out_specs=(grid, P("band", "domain")),
        check_vma=False,
    )

    def run(orbitals, potential):
        return body(orbitals, potential, jnp.asarray(high), jnp.asarray(low))

    return run
```

time: 723 us -> 219 us (0.30)
  waiting for transfers between devices: 453 us -> 0 us
  blocking collectives: 0 us -> 172 us
  local copies, waits for them, and re-layouts: 132 us -> 3.22 us
  other arithmetic: 82.5 us -> 0 us
  Pallas kernels: 0 us -> 41.9 us
  matrix products: 32.9 us -> 0 us
  between operations: 14.2 us -> 0.64 us
  starting transfers between devices: 8.13 us -> 0 us
    all_gather x1 -> x0, waiting for transfers between devices: 363 us -> none  [local(): lax.all_gather(flat, 'band', axis=1, tiled=True)]
    all_to_all x0 -> x4, blocking collectives: none -> 172 us  [the longest x2 80.3 us: local(): cells = lax.all_to_all(cells, 'domain', 0, 0, tiled=True)]
    slice x72 -> x0, local copies, waits for them, and re-layouts: 119 us -> none  [the longest x36 63.4 us: apply_ham(): cycle = cycle + jnp.roll(field, step, 2) + jnp.roll(field, -step, 2)]
    reduce_scatter x1 -> x0, waiting for transfers between devices: 67.3 us -> none  [local(): lax.psum_scatter(row_terms * (1.0 / cells_all), 'domain', scatter_dimensi...]
    sub x2 -> x0, other arithmetic: 54.4 us -> none  [local(): (apply_ham(current, potential) - center * current) * (2.0 * second / half...]
    pallas_call x0 -> x5, Pallas kernels: none -> 41.9 us  [call(): pl.pallas_call(kernel, out_shape=jax.ShapeDtypeStruct(shape, jnp.float32)...]
    dot_general x1 -> x0, matrix products: 32.9 us -> none  [inner_block(): lax.dot_general(left, right, (((0,), (0,)), ((), ())), precision=lax.Prec...]
    mul x2 -> x0, other arithmetic: 28.1 us -> none  [the longest x1 27.5 us: local(): (apply_ham(orbitals, potential) - center * orbitals) * (sigma / half_width)]
  transfers between devices with their start and end apart: 8 -> 0, of which waited for: 6 -> 0; matrix products, arithmetic and copies ran while one was open for 12% -> 0% of each run, Pallas kernels for 0% -> 0%
where the time goes in v1:
time: 219 us; the launch traced here: 218 us
  blocking collectives  172 us (79%)
  Pallas kernels  41.9 us (19%)
  local copies, waits for them, and re-layouts  3.22 us (1%)
    all_to_all x2, blocking collectives, local(): cells = lax.all_to_all(cells, 'domain', 0, 0, tiled=True)  80.3 us
    all_to_all x1, blocking collectives, local(): partial = lax.all_to_all(partial, ('band', 'domain'), 0, 0, tiled=True)  58.2 us
    pallas_call x5, Pallas kernels, call(): pl.pallas_call(kernel, out_shape=jax.ShapeDtypeStruct(shape, jnp.float32)...  41.9 us
    all_to_all x1, blocking collectives, local(): lax.all_to_all(flat.reshape(BANDS, PL * PTS // BANDS, OB), 'band', 0, 0,...  33.7 us

profile of v1, /device:TPU:0, one launch (start us, length us, event | category | flops | bytes accessed | tf_op | source)
XLA Modules:
  0.0 217.9 jit_solution(12999612284512609211)
XLA Ops:
  0.6 1.0 copy.8
  1.6 0.7 reshape.20.pot
  2.3 3.9 %shard_map.59 = f32[16,328,128]{2,1,0:T(8,128)} custom-call(f32[6,768,128]{2,1,0:T(8,128)} %bitcast.7, f32[36,128]{1,0:T(8,128)} %reshape.20.pot), custom_call_target="tpu_custom_call" | custom-call | tf_op jit(solution)/shard_map/pallas_call | solution.py:172
  6.2 43.8 %all_to_all.20.cells = f32[16,328,128]{2,1,0:T(8,128)} all-to-all(f32[16,328,128]{2,1,0:T(8,128)} %shard_map.59), channel_id=1, replica_groups=mesh['band'=8,'domain'=16] {'domain'}, dimensions={0} | all-to-all | bytes 5373952 | tf_op jit(solution)/shard_map/all_to_all | solution.py:187
  50.0 22.5 %shard_map.60 = f32[16,288,128]{2,1,0:T(8,128)} custom-call(f32[16,328,128]{2,1,0:T(8,128)} %all_to_all.20.cells, bf16[768,768]{1,0:T(8,128)(2,1)} %constant.4.clone.high, bf16[768,768]{1,0:T(8,128)(2,1)} %constant.5.clone.low), custom_call_target="tpu_custom_call" | custom-call | tf_op jit(solution)/shard_map/pallas_call | solution.py:172
  72.4 36.5 %all_to_all.21.cells = f32[16,288,128]{2,1,0:T(8,128)} all-to-all(f32[16,288,128]{2,1,0:T(8,128)} %shard_map.60), channel_id=1, replica_groups=mesh['band'=8,'domain'=16] {'domain'}, dimensions={0} | all-to-all | bytes 4718592 | tf_op jit(solution)/shard_map/all_to_all | solution.py:200
  108.9 3.7 %shard_map.61 = f32[4608,128]{1,0:T(8,128)} custom-call(f32[16,288,128]{2,1,0:T(8,128)} %all_to_all.21.cells), custom_call_target="tpu_custom_call" | custom-call | tf_op jit(solution)/shard_map/pallas_call | solution.py:172
  112.7 33.7 %all_to_all.22.cells = f32[8,576,128]{2,1,0:T(8,128)} all-to-all(f32[8,576,128]{2,1,0:T(8,128)} %bitcast.5), channel_id=1, replica_groups=mesh['band'=8,'domain'=16] {'band'}, dimensions={0} | all-to-all | bytes 4718592 | tf_op jit(solution)/shard_map/all_to_all | solution.py:202
  146.4 8.6 %shard_map.62 = f32[8,16,64,128]{3,2,1,0:T(8,128)} custom-call(f32[8,576,128]{2,1,0:T(8,128)} %all_to_all.22.cells), custom_call_target="tpu_custom_call" | custom-call | tf_op jit(solution)/shard_map/pallas_call | solution.py:172
  155.0 58.2 %all_to_all.23.parts = f32[128,64,128]{2,1,0:T(8,128)} all-to-all(f32[128,64,128]{2,1,0:T(8,128)} %bitcast.4), channel_id=1, replica_groups=mesh['band'=8,'domain'=16] {'band','domain'}, dimensions={0} | all-to-all | bytes 8388608 | tf_op jit(solution)/shard_map/all_to_all | solution.py:205
  213.2 3.2 %shard_map.63 = f32[128,64]{1,0:T(8,128)} custom-call(f32[128,64,128]{2,1,0:T(8,128)} %all_to_all.23.parts), custom_call_target="tpu_custom_call" | custom-call | tf_op jit(solution)/shard_map/pallas_call | solution.py:172
  216.4 1.5 copy.9

commit v2 on v1

v2 whole, which is shorter than its diff:
```python
import jax
import jax.numpy as jnp
import numpy as np
from jax import lax
from jax.experimental import pallas as pl
from jax.experimental.pallas import tpu as pltpu
from jax.sharding import PartitionSpec as P

DEG = 3

coeffs = (
    -5369.0 / 1800.0,
    12.0 / 7.0,
    -15.0 / 56.0,
    10.0 / 189.0,
    -1.0 / 112.0,
    2.0 / 1925.0,
    -1.0 / 16632.0,
)
bound_floor = 0.0
bound_cut = 2.0
bound_top = 11.0
center = (bound_top + bound_cut) / 2.0

NX, NY, NZ = 96, 32, 24
PTS = NY * NZ
LT = PTS // 128
BANDS, DOMS = 8, 16
PL = NX // DOMS
NORB = 1024
OB = NORB // BANDS
OD = OB // DOMS
ROWS = PL * LT * OD
POT = PL * LT
POT_PAD = 40
TURNS = 2
GRID = NX * PTS
MIB = 1024 * 1024


def steps():
    half_width = (bound_top - bound_cut) / 2.0
    sigma = half_width / (bound_floor - center)
    gamma = 2.0 / sigma
    scales, backs = [sigma / half_width], [0.0]
    for _ in range(2, DEG + 1):
        second = 1.0 / (gamma - sigma)
        scales.append(2.0 * second / half_width)
        backs.append(sigma * second)
        sigma = second
    out = [(0.0, 1.0)]
    for i in range(1, DEG):
        out.append((backs[i] / (scales[i] * scales[i - 1]), float(np.prod(scales)) if i == DEG - 1 else 1.0))
    return out


def plane_matrix():
    def ring(n):
        m = np.zeros((n, n))
        for k in range(1, 7):
            for i in range(n):
                m[i, (i + k) % n] += coeffs[k]
                m[i, (i - k) % n] += coeffs[k]
        return m

    m = np.kron(ring(NY), np.eye(NZ)) + np.kron(np.eye(NY), ring(NZ))
    m = -0.5 * (m + 3.0 * coeffs[0] * np.eye(PTS))
    hi = np.asarray(m, jnp.bfloat16)
    lo = np.asarray(m - hi.astype(np.float64), jnp.bfloat16)
    return hi, lo


def split(value):
    hi = value.astype(jnp.bfloat16)
    return hi, (value - hi.astype(jnp.float32)).astype(jnp.bfloat16)


def spread_kernel(cells, pot, out):
    for p in range(PL):
        flat = cells[p].T
        for j in range(LT):
            at = (p * LT + j) * OD
            out[:, at : at + OD, :] = flat[:, j * 128 : (j + 1) * 128].reshape(DOMS, OD, 128)
    turned = jnp.concatenate([(pot[p] - center).T for p in range(PL)], 0)
    spot = lax.broadcasted_iota(jnp.int32, (NZ, PTS), 1)
    pick = (lax.rem(spot, NZ) == lax.broadcasted_iota(jnp.int32, (NZ, PTS), 0)).astype(jnp.float32)
    wide = jnp.dot(turned, pick, precision=lax.Precision.HIGHEST, preferred_element_type=jnp.float32)
    point = lax.broadcasted_iota(jnp.int32, (NY, PTS), 1)
    first = lax.broadcasted_iota(jnp.int32, (NY, PTS), 0) * NZ
    keep = (point >= first) & (point < first + NZ)
    for p in range(PL):
        row = jnp.sum(jnp.where(keep, wide[p * NY : (p + 1) * NY, :], 0.0), 0, keepdims=True)
        for j in range(LT):
            at = ROWS + p * LT + j
            out[:, at : at + 1, :] = jnp.broadcast_to(row[None, :, j * 128 : (j + 1) * 128], (DOMS, 1, 128))
    out[:, ROWS + POT :, :] = jnp.zeros((DOMS, POT_PAD - POT, 128), jnp.float32)


def filter_kernel(cells, high, low, out, one, two, left_a, left_b, prod_a, prod_b):
    group = DOMS // TURNS
    at = [[slice((i * LT + j) * OD, (i * LT + j + 1) * OD) for i in range(PL)] for j in range(LT)]

    def keep(left, s, i, j, pair):
        rows = slice((s * PL + i - 1) * OD, (s * PL + i + 1) * OD)
        hi, lo = split(jnp.concatenate(pair, 0))
        left[rows, j * 128 : (j + 1) * 128] = hi
        left[rows, PTS + j * 128 : PTS + (j + 1) * 128] = lo

    def planes(left, prod, turn):
        rows = slice(turn * group * PL * OD, (turn + 1) * group * PL * OD)
        for n in range(PTS // 256):
            cols = slice(n * 256, (n + 1) * 256)
            prod[rows, cols] = (
                jnp.dot(left[rows, :PTS], high[:, cols], preferred_element_type=jnp.float32)
                + jnp.dot(left[rows, PTS:], high[:, cols], preferred_element_type=jnp.float32)
                + jnp.dot(left[rows, :PTS], low[:, cols], preferred_element_type=jnp.float32)
            )

    def across(cur, prior, new, prod, left, back, scale, turn):
        for s in range(turn * group, (turn + 1) * group):
            for j in range(LT):
                line = [cur[b % DOMS, at[j][i], :] for b in (s - 1, s, s + 1) for i in range(PL)]
                fresh = []
                for i in range(PL):
                    mid = PL + i
                    row = (s * PL + i) * OD
                    pot = cells[s, ROWS + i * LT + j, :][None]
                    total = prod[row : row + OD, j * 128 : (j + 1) * 128] + pot * line[mid]
                    for k in range(1, 7):
                        total = total + (-0.5 * coeffs[k]) * (line[mid + k] + line[mid - k])
                    if prior is not None:
                        total = total - back * prior[s, at[j][i], :]
                    if scale != 1.0:
                        total = total * scale
                    fresh.append(total)
                for i in range(PL):
                    new[s, at[j][i], :] = fresh[i]
                    if left is not None and i % 2:
                        keep(left, s, i, j, fresh[i - 1 : i + 1])

    for turn in range(TURNS):
        for s in range(turn * group, (turn + 1) * group):
            for j in range(LT):
                for i in range(1, PL, 2):
                    keep(left_a, s, i, j, [cells[s, at[j][i - 1], :], cells[s, at[j][i], :]])
        planes(left_a, prod_a, turn)
    values, lefts, prods = [cells, one, two, out], [left_a, left_b, left_a, None], [prod_a, prod_b, prod_a]
    for i, (back, scale) in enumerate(steps()):
        for turn in range(TURNS):
            across(values[i], values[i - 1] if i else None, values[i + 1], prods[i], lefts[i + 1], back, scale, turn)
            if i < DEG - 1:
                planes(lefts[i + 1], prods[i + 1], turn)


def gather_kernel(cells, out):
    for p in range(PL):
        for j in range(LT):
            at = (p * LT + j) * OD
            tile = cells[:, at : at + OD, :].reshape(OB, 128)
            out[p * PTS + j * 128 : p * PTS + (j + 1) * 128, :] = tile.T


def margin_kernel(cells, mine, others, left_hi, left_lo, right_hi, right_lo):
    wide = 2 * OB
    nd = NORB // DOMS
    even = lax.rem(lax.axis_index("core"), 2) == 0
    for b in range(BANDS):
        cols = slice(b * OB, (b + 1) * OB)
        right_hi[:, cols], right_lo[:, cols] = split(cells[b])
        left_hi[cols, :], left_lo[cols, :] = split(cells[b].T)

    def put(block, rows, cols):
        for c in range(2):
            for r in range(2):
                low = block[2 * r * nd : (2 * r + 1) * nd, c * OB : (c + 1) * OB]
                high = block[(2 * r + 1) * nd : (2 * r + 2) * nd, c * OB : (c + 1) * OB]
                mine[2 * cols + c, 2 * rows + r] = jnp.where(even, low, high)
                others[2 * cols + c, 2 * rows + r] = jnp.where(even, high, low)

    for i in range(NORB // wide):
        for j in range(i + 1):
            rows, cols = slice(i * wide, (i + 1) * wide), slice(j * wide, (j + 1) * wide)
            block = (
                jnp.dot(left_hi[rows, :], right_hi[:, cols], preferred_element_type=jnp.float32)
                + jnp.dot(left_lo[rows, :], right_hi[:, cols], preferred_element_type=jnp.float32)
                + jnp.dot(left_hi[rows, :], right_lo[:, cols], preferred_element_type=jnp.float32)
            )
            put(block, i, j)
            if i != j:
                put(block.T, j, i)


def sum_kernel(parts, out):
    total = parts[0]
    for i in range(1, BANDS * DOMS // 2):
        total = total + parts[i]
    out[...] = total * (1.0 / GRID)


def call(kernel, shape, *args, scratch=(), limit=16):
    shapes = shape if isinstance(shape, list) else [shape]
    out = [jax.ShapeDtypeStruct(s, jnp.float32) for s in shapes]
    return pl.pallas_call(
        kernel,
        out_shape=out if isinstance(shape, list) else out[0],
        scratch_shapes=list(scratch),
        compiler_params=pltpu.CompilerParams(vmem_limit_bytes=limit * MIB),
    )(*args)


BAND = ("x", "y_lo")
DOMAIN = ("y_hi", "z", "core")
CHIPS = ("x", "y_lo", "y_hi", "z")


def local(orbitals, potential, high, low):
    cells = call(
        spread_kernel,
        (DOMS, ROWS + POT_PAD, 128),
        orbitals.reshape(PL, PTS, OB),
        potential.transpose(0, 2, 1),
    )
    cells = lax.all_to_all(cells, DOMAIN, 0, 0, tiled=True)
    cells = call(
        filter_kernel,
        (DOMS, ROWS, 128),
        cells,
        high,
        low,
        scratch=[pltpu.VMEM((DOMS, ROWS, 128), jnp.float32)] * 2
        + [pltpu.VMEM((NX * OD, 2 * PTS), jnp.bfloat16)] * 2
        + [pltpu.VMEM((NX * OD, PTS), jnp.float32)] * 2,
        limit=32,
    )
    cells = lax.all_to_all(cells, DOMAIN, 0, 0, tiled=True)
    flat = call(gather_kernel, (PL * PTS, OB), cells)
    count = PL * PTS // BANDS
    points = lax.all_to_all(flat.reshape(BANDS, count, OB), BAND, 0, 0, tiled=True)
    shape = (BANDS, DOMS // 2, NORB // DOMS, OB)
    mine, others = call(
        margin_kernel,
        [shape, shape],
        points,
        scratch=[pltpu.VMEM((NORB, count), jnp.bfloat16)] * 2 + [pltpu.VMEM((count, NORB), jnp.bfloat16)] * 2,
        limit=24,
    )
    partial = mine + lax.ppermute(others, "core", [(0, 1), (1, 0)])
    partial = partial.reshape(BANDS * DOMS // 2, NORB // DOMS, OB)
    partial = lax.all_to_all(partial, CHIPS, 0, 0, tiled=True)
    margin = call(sum_kernel, (NORB // DOMS, OB), partial)
    return flat.reshape(PL, NY, NZ, OB), margin.T


def solution(mesh):
    mesh = jax.sharding.Mesh(mesh.devices.reshape(4, 2, 2, 4, 2), BAND + DOMAIN)
    grid, pot = P(DOMAIN, None, None, BAND), P(DOMAIN, None, None)
    high, low = plane_matrix()
    body = jax.shard_map(
        local,
        mesh=mesh,
        in_specs=(grid, pot, P(), P()),
        out_specs=(grid, P(BAND, DOMAIN)),
        check_vma=False,
    )

    def run(orbitals, potential):
        return body(orbitals, potential, jnp.asarray(high), jnp.asarray(low))

    return run
```

time: 219 us -> 174 us (0.79)
  blocking collectives: 172 us -> 147 us
  Pallas kernels: 41.9 us -> 18.9 us
  waiting for transfers between devices: 0 us -> 4.15 us
    all_to_all x4, blocking collectives: 172 us -> 147 us  [the longest x2 78.3 us: local(): cells = lax.all_to_all(cells, DOMAIN, 0, 0, tiled=True)]
    pallas_call x5, Pallas kernels: 41.9 us -> 18.9 us  [call(): pl.pallas_call(kernel, out_shape=out if isinstance(shape, list) else out[...]
    ppermute x0 -> x1, waiting for transfers between devices: none -> 4.15 us  [local(): partial = mine + lax.ppermute(others, 'core', [(0, 1), (1, 0)])]
  transfers between devices with their start and end apart: 0 -> 1, of which waited for: 0 -> 1; matrix products, arithmetic and copies ran while one was open for 0% -> 0% of each run, Pallas kernels for 0% -> 0%
where the time goes in v2:
time: 174 us; the launch traced here: 173 us
  blocking collectives  147 us (84%)
  Pallas kernels  18.9 us (11%)
  waiting for transfers between devices  4.15 us (2%)
  local copies, waits for them, and re-layouts  2.56 us (1%)
    all_to_all x2, blocking collectives, local(): cells = lax.all_to_all(cells, DOMAIN, 0, 0, tiled=True)  78.3 us
    all_to_all x1, blocking collectives, local(): partial = lax.all_to_all(partial, CHIPS, 0, 0, tiled=True)  34.9 us
    all_to_all x1, blocking collectives, local(): lax.all_to_all(flat.reshape(BANDS, count, OB), BAND, 0, 0, tiled=True)  33.5 us
    pallas_call x5, Pallas kernels, call(): pl.pallas_call(kernel, out_shape=out if isinstance(shape, list) else out[...  18.9 us
    ppermute x1, waiting for transfers between devices, local(): partial = mine + lax.ppermute(others, 'core', [(0, 1), (1, 0)])  4.15 us
  transfers between devices with their start and end apart: 1, of which 1 were waited for; matrix products, arithmetic and copies ran while one was open for 0% of the time, Pallas kernels for 0%

profile of v2, /device:TPU:0, one launch (start us, length us, event | category | flops | bytes accessed | tf_op | source)
XLA Modules:
  0.0 173.4 jit_solution(9763481832336864739)
XLA Ops:
  0.6 0.0 copy-start
  0.6 1.7 copy-done
  2.3 0.0 copy-start.3
  2.3 0.9 copy-done.3
  3.2 0.8 shard_map.59
  4.0 0.0 copy-start.1
  4.0 0.0 copy-start.2
  4.0 43.6 %all_to_all.20.cells = f32[16,328,128]{2,1,0:T(8,128)S(1)} all-to-all(f32[16,328,128]{2,1,0:T(8,128)S(1)} %shard_map.59), channel_id=1, replica_groups=mesh['x'=4,'y_lo'=2,'y_hi'=2,'z'=4,'core'=2] {'y_hi','z','core'}, dimensions={0} | all-to-all | bytes 5373952 | tf_op jit(solution)/shard_map/all_to_all | solution.py:223
  47.7 0.0 copy-done.1
  47.7 0.0 copy-done.2
  47.7 11.7 %shard_map.60 = f32[16,288,128]{2,1,0:T(8,128)S(1)} custom-call(f32[16,328,128]{2,1,0:T(8,128)S(1)} %all_to_all.20.cells, bf16[768,768]{1,0:T(8,128)(2,1)S(1)} %copy-done.2, bf16[768,768]{1,0:T(8,128)(2,1)S(1)} %copy-done.1), custom_call_target="tpu_custom_call" | custom-call | tf_op jit(solution)/shard_map/pallas_call | solution.py:203
  59.3 34.6 %all_to_all.21.cells = f32[16,288,128]{2,1,0:T(8,128)S(1)} all-to-all(f32[16,288,128]{2,1,0:T(8,128)S(1)} %shard_map.60), channel_id=1, replica_groups=mesh['x'=4,'y_lo'=2,'y_hi'=2,'z'=4,'core'=2] {'y_hi','z','core'}, dimensions={0} | all-to-all | bytes 4718592 | tf_op jit(solution)/shard_map/all_to_all | solution.py:235
  94.0 2.1 %shard_map.61 = f32[4608,128]{1,0:T(8,128)} custom-call(f32[16,288,128]{2,1,0:T(8,128)S(1)} %all_to_all.21.cells), custom_call_target="tpu_custom_call" | custom-call | tf_op jit(solution)/shard_map/pallas_call | solution.py:203
  96.1 33.5 %all_to_all.22.cells = f32[8,576,128]{2,1,0:T(8,128)S(1)} all-to-all(f32[8,576,128]{2,1,0:T(8,128)} %bitcast.8), channel_id=1, replica_groups=mesh['x'=4,'y_lo'=2,'y_hi'=2,'z'=4,'core'=2] {'x','y_lo'}, dimensions={0} | all-to-all | bytes 4718592 | tf_op jit(solution)/shard_map/all_to_all | solution.py:238
  129.6 3.5 %shard_map.62 = (f32[8,8,64,128]{3,2,1,0:T(8,128)S(1)}, f32[8,8,64,128]{3,2,1,0:T(8,128)S(1)}) custom-call(f32[8,576,128]{2,1,0:T(8,128)S(1)} %all_to_all.22.cells), custom_call_target="tpu_custom_call" | custom-call | tf_op jit(solution)/shard_map/pallas_call | solution.py:203
  133.1 0.1 collective-permute-start
  133.2 4.1 %collective-permute-done = f32[8,8,64,128]{3,2,1,0:T(8,128)S(1)} collective-permute-done((f32[8,8,64,128]{3,2,1,0:T(8,128)S(1)}, f32[8,8,64,128]{3,2,1,0:T(8,128)S(1)}, u32[]{:S(2)}, u32[]{:S(2)}) %collective-permute-start) | collective-permute-done | bytes 2097184 | tf_op jit(solution)/shard_map/ppermute | solution.py:247
  137.3 0.4 add.3
  137.7 34.9 %all_to_all.23.parts = f32[64,64,128]{2,1,0:T(8,128)S(1)} all-to-all(f32[64,64,128]{2,1,0:T(8,128)S(1)} %bitcast.10), channel_id=1, replica_groups=mesh['x'=4,'y_lo'=2,'y_hi'=2,'z'=4,'core'=2] {'x','y_lo','y_hi','z'}, dimensions={0} | all-to-all | bytes 4194304 | tf_op jit(solution)/shard_map/all_to_all | solution.py:249
  172.6 0.8 shard_map.63
Async XLA Ops:
  0.6 1.7 copy-start
  2.3 0.9 copy-start.3
  4.0 43.7 %copy-start.1 = (bf16[768,768]{1,0:T(8,128)(2,1)S(1)}, bf16[768,768]{1,0:T(8,128)(2,1)}, u32[]{:S(2)}) copy-start(bf16[768,768]{1,0:T(8,128)(2,1)} %constant.5.clone.low) | copy-start | bytes 3538948
  4.0 43.6 %copy-start.2 = (bf16[768,768]{1,0:T(8,128)(2,1)S(1)}, bf16[768,768]{1,0:T(8,128)(2,1)}, u32[]{:S(2)}) copy-start(bf16[768,768]{1,0:T(8,128)(2,1)} %constant.4.clone.high) | copy-start | bytes 3538948
  133.1 4.2 %collective-permute-start = (f32[8,8,64,128]{3,2,1,0:T(8,128)S(1)}, f32[8,8,64,128]{3,2,1,0:T(8,128)S(1)}, u32[]{:S(2)}, u32[]{:S(2)}) collective-permute-start(f32[8,8,64,128]{3,2,1,0:T(8,128)S(1)} %get-tuple-element.5), channel_id=1, source_target_pairs={{0,1},{1,0},{2,3},{3,2},{4,5},{5,4},{6,7},{7,6},{8,9},{9,8},{10,11... | collective-permute-start | bytes 6291464 | tf_op jit(solution)/shard_map/ppermute | solution.py:247

commit v3 on v2

--- a/solution.py
+++ b/solution.py
@@ -75,12 +75,13 @@
     return hi, (value - hi.astype(jnp.float32)).astype(jnp.bfloat16)
 
 
-def spread_kernel(cells, pot, out):
-    for p in range(PL):
-        flat = cells[p].T
-        for j in range(LT):
-            at = (p * LT + j) * OD
-            out[:, at : at + OD, :] = flat[:, j * 128 : (j + 1) * 128].reshape(DOMS, OD, 128)
+def spread_kernel(cells, out):
+    flat = cells[0].T
+    for j in range(LT):
+        out[:, j * OD : (j + 1) * OD, :] = flat[:, j * 128 : (j + 1) * 128].reshape(DOMS, OD, 128)
+
+
+def potential_kernel(pot, out):
     turned = jnp.concatenate([(pot[p] - center).T for p in range(PL)], 0)
     spot = lax.broadcasted_iota(jnp.int32, (NZ, PTS), 1)
     pick = (lax.rem(spot, NZ) == lax.broadcasted_iota(jnp.int32, (NZ, PTS), 0)).astype(jnp.float32)
@@ -91,12 +92,12 @@
     for p in range(PL):
         row = jnp.sum(jnp.where(keep, wide[p * NY : (p + 1) * NY, :], 0.0), 0, keepdims=True)
         for j in range(LT):
-            at = ROWS + p * LT + j
-            out[:, at : at + 1, :] = jnp.broadcast_to(row[None, :, j * 128 : (j + 1) * 128], (DOMS, 1, 128))
-    out[:, ROWS + POT :, :] = jnp.zeros((DOMS, POT_PAD - POT, 128), jnp.float32)
-
-
-def filter_kernel(cells, high, low, out, one, two, left_a, left_b, prod_a, prod_b):
+            at = p * LT + j
+            out[at : at + 1, :] = row[:, j * 128 : (j + 1) * 128]
+    out[POT:, :] = jnp.zeros((POT_PAD - POT, 128), jnp.float32)
+
+
+def filter_kernel(cells, field, high, low, out, one, two, left_a, left_b, prod_a, prod_b):
     group = DOMS // TURNS
     at = [[slice((i * LT + j) * OD, (i * LT + j + 1) * OD) for i in range(PL)] for j in range(LT)]
 
@@ -124,7 +125,7 @@
                 for i in range(PL):
                     mid = PL + i
                     row = (s * PL + i) * OD
-                    pot = cells[s, ROWS + i * LT + j, :][None]
+                    pot = field[s, i * LT + j, :][None]
                     total = prod[row : row + OD, j * 128 : (j + 1) * 128] + pot * line[mid]
                     for k in range(1, 7):
                         total = total + (-0.5 * coeffs[k]) * (line[mid + k] + line[mid - k])
@@ -153,11 +154,10 @@
 
 
 def gather_kernel(cells, out):
-    for p in range(PL):
-        for j in range(LT):
-            at = (p * LT + j) * OD
-            tile = cells[:, at : at + OD, :].reshape(OB, 128)
-            out[p * PTS + j * 128 : p * PTS + (j + 1) * 128, :] = tile.T
+    start = pl.multiple_of(pl.program_id(0) * (LT * OD), LT * OD)
+    for j in range(LT):
+        tile = cells[:, pl.ds(start + j * OD, OD), :].reshape(OB, 128)
+        out[j * 128 : (j + 1) * 128, :] = tile.T
 
 
 def margin_kernel(cells, mine, others, left_hi, left_lo, right_hi, right_lo):
@@ -214,26 +214,34 @@
 
 
 def local(orbitals, potential, high, low):
-    cells = call(
+    cells = pl.pallas_call(
         spread_kernel,
-        (DOMS, ROWS + POT_PAD, 128),
-        orbitals.reshape(PL, PTS, OB),
-        potential.transpose(0, 2, 1),
-    )
+        grid=(PL,),
+        out_shape=jax.ShapeDtypeStruct((DOMS, ROWS, 128), jnp.float32),
+        in_specs=[pl.BlockSpec((1, PTS, OB), lambda p: (p, 0, 0))],
+        out_specs=pl.BlockSpec((DOMS, LT * OD, 128), lambda p: (0, p, 0)),
+        compiler_params=pltpu.CompilerParams(vmem_limit_bytes=60 * MIB),
+    )(orbitals.reshape(PL, PTS, OB))
+    field = call(potential_kernel, (POT_PAD, 128), potential.transpose(0, 2, 1))
+    field = lax.all_gather(field, DOMAIN)
     cells = lax.all_to_all(cells, DOMAIN, 0, 0, tiled=True)
-    cells = call(
+    cells = pl.pallas_call(
         filter_kernel,
-        (DOMS, ROWS, 128),
-        cells,
-        high,
-        low,
-        scratch=[pltpu.VMEM((DOMS, ROWS, 128), jnp.float32)] * 2
+        out_shape=jax.ShapeDtypeStruct((DOMS, ROWS, 128), jnp.float32),
+        scratch_shapes=[pltpu.VMEM((DOMS, ROWS, 128), jnp.float32)] * 2
         + [pltpu.VMEM((NX * OD, 2 * PTS), jnp.bfloat16)] * 2
         + [pltpu.VMEM((NX * OD, PTS), jnp.float32)] * 2,
-        limit=32,
-    )
+        compiler_params=pltpu.CompilerParams(vmem_limit_bytes=48 * MIB),
+    )(cells, field, high, low)
     cells = lax.all_to_all(cells, DOMAIN, 0, 0, tiled=True)
-    flat = call(gather_kernel, (PL * PTS, OB), cells)
+    flat = pl.pallas_call(
+        gather_kernel,
+        grid=(PL,),
+        out_shape=jax.ShapeDtypeStruct((PL * PTS, OB), jnp.float32),
+        in_specs=[pl.BlockSpec(memory_space=pltpu.VMEM)],
+        out_specs=pl.BlockSpec((PTS, OB), lambda p: (p, 0)),
+        compiler_params=pltpu.CompilerParams(vmem_limit_bytes=16 * MIB),
+    )(cells)
     count = PL * PTS // BANDS
     points = lax.all_to_all(flat.reshape(BANDS, count, OB), BAND, 0, 0, tiled=True)
     shape = (BANDS, DOMS // 2, NORB // DOMS, OB)

time: 174 us -> 191 us (1.098)
  starting transfers between devices: 0.09 us -> 8.4 us
  Pallas kernels: 18.9 us -> 26.6 us
  blocking collectives: 147 us -> 151 us
  local copies, waits for them, and re-layouts: 2.56 us -> 0.01 us
    all_gather x0 -> x1, blocking collectives: none -> 46.1 us  [local(): field = lax.all_gather(field, DOMAIN)]
    all_to_all x2 -> x1, blocking collectives: 78.3 us -> 35 us  [local(): cells = lax.all_to_all(cells, DOMAIN, 0, 0, tiled=True)]
    pallas_call x0 -> x3, Pallas kernels: none -> 21.6 us  [the longest x1 13.4 us: local(): pl.pallas_call(filter_kernel, out_shape=jax.ShapeDtypeStruct((DOMS, ROWS,...]
    pallas_call x5 -> x3, Pallas kernels: 18.9 us -> 4.97 us  [call(): pl.pallas_call(kernel, out_shape=out if isinstance(shape, list) else out[...]
    all_to_all x0 -> x1, starting transfers between devices: none -> 8.32 us  [local(): cells = lax.all_to_all(cells, DOMAIN, 0, 0, tiled=True)]
    unnamed x8 -> x6, local copies, waits for them, and re-layouts: 2.56 us -> 0.01 us
  transfers between devices with their start and end apart: 1 -> 2, of which waited for: 1 -> 1; matrix products, arithmetic and copies ran while one was open for 0% -> 0% of each run, Pallas kernels for 0% -> 0%
where the time goes in v3:
time: 191 us
  blocking collectives  151 us (79%)
  Pallas kernels  26.6 us (14%)
  starting transfers between devices  8.4 us (4%)
  waiting for transfers between devices  4.15 us (2%)
    all_gather x1, blocking collectives, local(): field = lax.all_gather(field, DOMAIN)  46.1 us
    all_to_all x1, blocking collectives, local(): cells = lax.all_to_all(cells, DOMAIN, 0, 0, tiled=True)  35 us
    all_to_all x1, blocking collectives, local(): partial = lax.all_to_all(partial, CHIPS, 0, 0, tiled=True)  34.9 us
    all_to_all x1, blocking collectives, local(): lax.all_to_all(flat.reshape(BANDS, count, OB), BAND, 0, 0, tiled=True)  34.4 us
    pallas_call x1, Pallas kernels, local(): pl.pallas_call(filter_kernel, out_shape=jax.ShapeDtypeStruct((DOMS, ROWS,...  13.4 us
    all_to_all x1, starting transfers between devices, local(): cells = lax.all_to_all(cells, DOMAIN, 0, 0, tiled=True)  8.32 us
    pallas_call x1, Pallas kernels, local(): pl.pallas_call(spread_kernel, grid=(PL,), out_shape=jax.ShapeDtypeStruct(...  5.31 us
    pallas_call x3, Pallas kernels, call(): pl.pallas_call(kernel, out_shape=out if isinstance(shape, list) else out[...  4.97 us
  transfers between devices with their start and end apart: 2, of which 1 were waited for; matrix products, arithmetic and copies ran while one was open for 0% of the time, Pallas kernels for 0%

profile of v3, /device:TPU:0, one launch (start us, length us, event | category | flops | bytes accessed | tf_op | source)
XLA Modules:
  0.0 190.7 jit_solution(1483643110177217652)
XLA Ops:
  0.6 5.3 %shard_map.59 = f32[16,288,128]{2,1,0:T(8,128)} custom-call(f32[6,768,128]{2,1,0:T(8,128)} %bitcast.12), custom_call_target="tpu_custom_call" | custom-call | tf_op jit(solution)/shard_map/pallas_call | solution.py:217
  5.9 0.0 copy-start.2
  5.9 0.0 copy-start
  5.9 0.0 copy-start.1
  5.9 8.3 %all-to-all-start = ((f32[16,288,128]{2,1,0:T(8,128)}), f32[16,288,128]{2,1,0:T(8,128)}, u32[]{:S(2)}, u32[]{:S(2)}) async-start(f32[16,288,128]{2,1,0:T(8,128)} %shard_map.59), calls=%async_computation | async-start | bytes 4718592 | tf_op jit(solution)/shard_map/all_to_all | solution.py:227
  14.3 0.0 copy-done.2
  14.3 0.7 shard_map.60
  15.0 46.1 %all-gather = f32[640,128]{1,0:T(8,128)S(1)} all-gather(f32[40,128]{1,0:T(8,128)S(1)} %shard_map.60), channel_id=2, replica_groups=mesh['x'=4,'y_lo'=2,'y_hi'=2,'z'=4,'core'=2] {'y_hi','z','core'}, dimensions={0}, use_global_device_ids=true | all-gather | bytes 348160 | tf_op jit(solution)/shard_map/all_gather | solution.py:226
  61.1 0.0 all-to-all-done.cells
  61.1 0.0 copy-done
  61.1 0.0 copy-done.1
  61.1 13.4 %shard_map.61 = f32[16,288,128]{2,1,0:T(8,128)S(1)} custom-call(f32[16,288,128]{2,1,0:T(8,128)} %all-to-all-done.cells, f32[16,40,128]{2,1,0:T(8,128)S(1)} %bitcast.7, bf16[768,768]{1,0:T(8,128)(2,1)S(1)} %copy-done.1, bf16[768,768]{1,0:T(8,128)(2,1)S(1)} %copy-done), custom_call_target="tpu_custom_call" | custom-call | tf_op jit(solution)/shard_map/pallas_call | solution.py:228
  74.5 35.0 %all_to_all.20.cells = f32[16,288,128]{2,1,0:T(8,128)S(1)} all-to-all(f32[16,288,128]{2,1,0:T(8,128)S(1)} %shard_map.61), channel_id=1, replica_groups=mesh['x'=4,'y_lo'=2,'y_hi'=2,'z'=4,'core'=2] {'y_hi','z','core'}, dimensions={0} | all-to-all | bytes 4718592 | tf_op jit(solution)/shard_map/all_to_all | solution.py:236
  109.5 2.9 %shard_map.62 = f32[4608,128]{1,0:T(8,128)} custom-call(f32[16,288,128]{2,1,0:T(8,128)S(1)} %all_to_all.20.cells), custom_call_target="tpu_custom_call" | custom-call | tf_op jit(solution)/shard_map/pallas_call | solution.py:237
  112.4 34.4 %all_to_all.21.cells = f32[8,576,128]{2,1,0:T(8,128)S(1)} all-to-all(f32[8,576,128]{2,1,0:T(8,128)} %bitcast.9), channel_id=1, replica_groups=mesh['x'=4,'y_lo'=2,'y_hi'=2,'z'=4,'core'=2] {'x','y_lo'}, dimensions={0} | all-to-all | bytes 4718592 | tf_op jit(solution)/shard_map/all_to_all | solution.py:246
  146.8 3.5 %shard_map.63 = (f32[8,8,64,128]{3,2,1,0:T(8,128)S(1)}, f32[8,8,64,128]{3,2,1,0:T(8,128)S(1)}) custom-call(f32[8,576,128]{2,1,0:T(8,128)S(1)} %all_to_all.21.cells), custom_call_target="tpu_custom_call" | custom-call | tf_op jit(solution)/shard_map/pallas_call | solution.py:203
  150.4 0.1 collective-permute-start
  150.5 4.1 %collective-permute-done = f32[8,8,64,128]{3,2,1,0:T(8,128)S(1)} collective-permute-done((f32[8,8,64,128]{3,2,1,0:T(8,128)S(1)}, f32[8,8,64,128]{3,2,1,0:T(8,128)S(1)}, u32[]{:S(2)}, u32[]{:S(2)}) %collective-permute-start) | collective-permute-done | bytes 2097184 | tf_op jit(solution)/shard_map/ppermute | solution.py:255
  154.6 0.4 add.3
  155.0 34.9 %all_to_all.22.parts = f32[64,64,128]{2,1,0:T(8,128)S(1)} all-to-all(f32[64,64,128]{2,1,0:T(8,128)S(1)} %bitcast.11), channel_id=1, replica_groups=mesh['x'=4,'y_lo'=2,'y_hi'=2,'z'=4,'core'=2] {'x','y_lo','y_hi','z'}, dimensions={0} | all-to-all | bytes 4194304 | tf_op jit(solution)/shard_map/all_to_all | solution.py:257
  190.0 0.8 shard_map.64
Async XLA Ops:
  5.9 8.3 %copy-start.2 = (f32[6,32,24]{1,2,0:T(8,128)S(1)}, f32[6,32,24]{1,2,0:T(8,128)}, u32[]{:S(2)}) copy-start(f32[6,32,24]{1,2,0:T(8,128)} %param.5) | copy-start | bytes 55300
  5.9 55.1 %copy-start = (bf16[768,768]{1,0:T(8,128)(2,1)S(1)}, bf16[768,768]{1,0:T(8,128)(2,1)}, u32[]{:S(2)}) copy-start(bf16[768,768]{1,0:T(8,128)(2,1)} %constant.5.clone.low) | copy-start | bytes 3538948
  5.9 55.1 %copy-start.1 = (bf16[768,768]{1,0:T(8,128)(2,1)S(1)}, bf16[768,768]{1,0:T(8,128)(2,1)}, u32[]{:S(2)}) copy-start(bf16[768,768]{1,0:T(8,128)(2,1)} %constant.4.clone.high) | copy-start | bytes 3538948
  5.9 55.1 %all-to-all-start = ((f32[16,288,128]{2,1,0:T(8,128)}), f32[16,288,128]{2,1,0:T(8,128)}, u32[]{:S(2)}, u32[]{:S(2)}) async-start(f32[16,288,128]{2,1,0:T(8,128)} %shard_map.59), calls=%async_computation | async-start | bytes 4718592 | tf_op jit(solution)/shard_map/all_to_all | solution.py:227
  150.4 4.2 %collective-permute-start = (f32[8,8,64,128]{3,2,1,0:T(8,128)S(1)}, f32[8,8,64,128]{3,2,1,0:T(8,128)S(1)}, u32[]{:S(2)}, u32[]{:S(2)}) collective-permute-start(f32[8,8,64,128]{3,2,1,0:T(8,128)S(1)} %get-tuple-element.5), channel_id=1, source_target_pairs={{0,1},{1,0},{2,3},{3,2},{4,5},{5,4},{6,7},{7,6},{8,9},{9,8},{10,11... | collective-permute-start | bytes 6291464 | tf_op jit(solution)/shard_map/ppermute | solution.py:255

commit v4 on v2

--- a/solution.py
+++ b/solution.py
@@ -38,14 +38,18 @@
 MIB = 1024 * 1024
 
 
+STRETCH = 35.0 / 16.0
+along = [-0.5 * STRETCH * c for c in coeffs]
+
+
 def steps():
     half_width = (bound_top - bound_cut) / 2.0
     sigma = half_width / (bound_floor - center)
     gamma = 2.0 / sigma
-    scales, backs = [sigma / half_width], [0.0]
+    scales, backs = [sigma / half_width / STRETCH], [0.0]
     for _ in range(2, DEG + 1):
         second = 1.0 / (gamma - sigma)
-        scales.append(2.0 * second / half_width)
+        scales.append(2.0 * second / half_width / STRETCH)
         backs.append(sigma * second)
         sigma = second
     out = [(0.0, 1.0)]
@@ -59,15 +63,11 @@
         m = np.zeros((n, n))
         for k in range(1, 7):
             for i in range(n):
-                m[i, (i + k) % n] += coeffs[k]
-                m[i, (i - k) % n] += coeffs[k]
+                m[i, (i + k) % n] += along[k]
+                m[i, (i - k) % n] += along[k]
         return m
 
-    m = np.kron(ring(NY), np.eye(NZ)) + np.kron(np.eye(NY), ring(NZ))
-    m = -0.5 * (m + 3.0 * coeffs[0] * np.eye(PTS))
-    hi = np.asarray(m, jnp.bfloat16)
-    lo = np.asarray(m - hi.astype(np.float64), jnp.bfloat16)
-    return hi, lo
+    return np.asarray(np.kron(ring(NY), np.eye(NZ)) + np.kron(np.eye(NY), ring(NZ)), jnp.bfloat16)
 
 
 def split(value):
@@ -81,7 +81,7 @@
         for j in range(LT):
             at = (p * LT + j) * OD
             out[:, at : at + OD, :] = flat[:, j * 128 : (j + 1) * 128].reshape(DOMS, OD, 128)
-    turned = jnp.concatenate([(pot[p] - center).T for p in range(PL)], 0)
+    turned = jnp.concatenate([(STRETCH * (pot[p] - center) + 3.0 * along[0]).T for p in range(PL)], 0)
     spot = lax.broadcasted_iota(jnp.int32, (NZ, PTS), 1)
     pick = (lax.rem(spot, NZ) == lax.broadcasted_iota(jnp.int32, (NZ, PTS), 0)).astype(jnp.float32)
     wide = jnp.dot(turned, pick, precision=lax.Precision.HIGHEST, preferred_element_type=jnp.float32)
@@ -96,7 +96,7 @@
     out[:, ROWS + POT :, :] = jnp.zeros((DOMS, POT_PAD - POT, 128), jnp.float32)
 
 
-def filter_kernel(cells, high, low, out, one, two, left_a, left_b, prod_a, prod_b):
+def filter_kernel(cells, ring, out, one, two, left_a, left_b, prod_a, prod_b):
     group = DOMS // TURNS
     at = [[slice((i * LT + j) * OD, (i * LT + j + 1) * OD) for i in range(PL)] for j in range(LT)]
 
@@ -111,9 +111,8 @@
         for n in range(PTS // 256):
             cols = slice(n * 256, (n + 1) * 256)
             prod[rows, cols] = (
-                jnp.dot(left[rows, :PTS], high[:, cols], preferred_element_type=jnp.float32)
-                + jnp.dot(left[rows, PTS:], high[:, cols], preferred_element_type=jnp.float32)
-                + jnp.dot(left[rows, :PTS], low[:, cols], preferred_element_type=jnp.float32)
+                jnp.dot(left[rows, :PTS], ring[:, cols], preferred_element_type=jnp.float32)
+                + jnp.dot(left[rows, PTS:], ring[:, cols], preferred_element_type=jnp.float32)
             )
 
     def across(cur, prior, new, prod, left, back, scale, turn):
@@ -127,7 +126,7 @@
                     pot = cells[s, ROWS + i * LT + j, :][None]
                     total = prod[row : row + OD, j * 128 : (j + 1) * 128] + pot * line[mid]
                     for k in range(1, 7):
-                        total = total + (-0.5 * coeffs[k]) * (line[mid + k] + line[mid - k])
+                        total = total + along[k] * (line[mid + k] + line[mid - k])
                     if prior is not None:
                         total = total - back * prior[s, at[j][i], :]
                     if scale != 1.0:
@@ -160,34 +159,51 @@
             out[p * PTS + j * 128 : p * PTS + (j + 1) * 128, :] = tile.T
 
 
-def margin_kernel(cells, mine, others, left_hi, left_lo, right_hi, right_lo):
+def margin_blocks(parts, mine, others, pairs):
+    left_hi, left_lo, right_hi, right_lo = parts
     wide = 2 * OB
     nd = NORB // DOMS
     even = lax.rem(lax.axis_index("core"), 2) == 0
+
+    def put(block, i, j):
+        for c in range(2):
+            for r in range(2):
+                first = block[2 * r * nd : (2 * r + 1) * nd, c * OB : (c + 1) * OB]
+                second = block[(2 * r + 1) * nd : (2 * r + 2) * nd, c * OB : (c + 1) * OB]
+                at = (j // 2, 2 * (j % 2) + c, 2 * (i % 2) + r)
+                mine[at] = jnp.where(even, first, second)
+                others[at] = jnp.where(even, second, first)
+
+    for i, j in pairs:
+        rows, cols = slice(i * wide, (i + 1) * wide), slice(j * wide, (j + 1) * wide)
+        block = (
+            jnp.dot(left_hi[rows, :], right_hi[:, cols], preferred_element_type=jnp.float32)
+            + jnp.dot(left_lo[rows, :], right_hi[:, cols], preferred_element_type=jnp.float32)
+            + jnp.dot(left_hi[rows, :], right_lo[:, cols], preferred_element_type=jnp.float32)
+        )
+        put(block, i, j)
+        if i != j:
+            put(block.T, j, i)
+
+
+def far_kernel(cells, mine, others, left_hi, left_lo, right_hi, right_lo):
     for b in range(BANDS):
         cols = slice(b * OB, (b + 1) * OB)
         right_hi[:, cols], right_lo[:, cols] = split(cells[b])
         left_hi[cols, :], left_lo[cols, :] = split(cells[b].T)
-
-    def put(block, rows, cols):
-        for c in range(2):
-            for r in range(2):
-                low = block[2 * r * nd : (2 * r + 1) * nd, c * OB : (c + 1) * OB]
-                high = block[(2 * r + 1) * nd : (2 * r + 2) * nd, c * OB : (c + 1) * OB]
-                mine[2 * cols + c, 2 * rows + r] = jnp.where(even, low, high)
-                others[2 * cols + c, 2 * rows + r] = jnp.where(even, high, low)
-
-    for i in range(NORB // wide):
-        for j in range(i + 1):
-            rows, cols = slice(i * wide, (i + 1) * wide), slice(j * wide, (j + 1) * wide)
-            block = (
-                jnp.dot(left_hi[rows, :], right_hi[:, cols], preferred_element_type=jnp.float32)
-                + jnp.dot(left_lo[rows, :], right_hi[:, cols], preferred_element_type=jnp.float32)
-                + jnp.dot(left_hi[rows, :], right_lo[:, cols], preferred_element_type=jnp.float32)
-            )
-            put(block, i, j)
-            if i != j:
-                put(block.T, j, i)
+    margin_blocks((left_hi, left_lo, right_hi, right_lo), mine, others, [(2, 0), (3, 0), (2, 1), (3, 1)])
+
+
+def near_kernel(left_hi, left_lo, right_hi, right_lo, mine, others):
+    parts = (left_hi, left_lo, right_hi, right_lo)
+    margin_blocks(parts, mine, others, [(0, 0), (1, 0), (1, 1), (2, 2), (3, 2), (3, 3)])
+
+
+def join_kernel(far, far_other, near, near_other, out):
+    for h in range(2):
+        here, there = slice(4 * h, 4 * h + 4), slice(4 - 4 * h, 8 - 4 * h)
+        out[here, there] = far[h] + far_other[h]
+        out[here, here] = near[h] + near_other[h]
 
 
 def sum_kernel(parts, out):
@@ -213,7 +229,7 @@
 CHIPS = ("x", "y_lo", "y_hi", "z")
 
 
-def local(orbitals, potential, high, low):
+def local(orbitals, potential, ring):
     cells = call(
         spread_kernel,
         (DOMS, ROWS + POT_PAD, 128),
@@ -225,8 +241,7 @@
         filter_kernel,
         (DOMS, ROWS, 128),
         cells,
-        high,
-        low,
+        ring,
         scratch=[pltpu.VMEM((DOMS, ROWS, 128), jnp.float32)] * 2
         + [pltpu.VMEM((NX * OD, 2 * PTS), jnp.bfloat16)] * 2
         + [pltpu.VMEM((NX * OD, PTS), jnp.float32)] * 2,
@@ -236,15 +251,16 @@
     flat = call(gather_kernel, (PL * PTS, OB), cells)
     count = PL * PTS // BANDS
     points = lax.all_to_all(flat.reshape(BANDS, count, OB), BAND, 0, 0, tiled=True)
-    shape = (BANDS, DOMS // 2, NORB // DOMS, OB)
-    mine, others = call(
-        margin_kernel,
-        [shape, shape],
-        points,
-        scratch=[pltpu.VMEM((NORB, count), jnp.bfloat16)] * 2 + [pltpu.VMEM((count, NORB), jnp.bfloat16)] * 2,
-        limit=24,
-    )
-    partial = mine + lax.ppermute(others, "core", [(0, 1), (1, 0)])
+    shape = (2, BANDS // 2, DOMS // 4, NORB // DOMS, OB)
+    half = (jax.ShapeDtypeStruct(shape, jnp.float32),) * 2
+    parts = (jax.ShapeDtypeStruct((NORB, count), jnp.bfloat16),) * 2
+    parts += (jax.ShapeDtypeStruct((count, NORB), jnp.bfloat16),) * 2
+    limits = pltpu.CompilerParams(vmem_limit_bytes=16 * MIB)
+    far, far_other, *parts = pl.pallas_call(far_kernel, out_shape=half + parts, compiler_params=limits)(points)
+    far_other = lax.ppermute(far_other, "core", [(0, 1), (1, 0)])
+    near, near_other = pl.pallas_call(near_kernel, out_shape=half, compiler_params=limits)(*parts)
+    near_other = lax.ppermute(near_other, "core", [(0, 1), (1, 0)])
+    partial = call(join_kernel, (BANDS, DOMS // 2, NORB // DOMS, OB), far, far_other, near, near_other)
     partial = partial.reshape(BANDS * DOMS // 2, NORB // DOMS, OB)
     partial = lax.all_to_all(partial, CHIPS, 0, 0, tiled=True)
     margin = call(sum_kernel, (NORB // DOMS, OB), partial)
@@ -254,16 +270,16 @@
 def solution(mesh):
     mesh = jax.sharding.Mesh(mesh.devices.reshape(4, 2, 2, 4, 2), BAND + DOMAIN)
     grid, pot = P(DOMAIN, None, None, BAND), P(DOMAIN, None, None)
-    high, low = plane_matrix()
+    ring = plane_matrix()
     body = jax.shard_map(
         local,
         mesh=mesh,
-        in_specs=(grid, pot, P(), P()),
+        in_specs=(grid, pot, P()),
         out_specs=(grid, P(BAND, DOMAIN)),
         check_vma=False,
     )
 
     def run(orbitals, potential):
-        return body(orbitals, potential, jnp.asarray(high), jnp.asarray(low))
+        return body(orbitals, potential, jnp.asarray(ring))
 
     return run

time: 174 us -> 171 us (0.983)
  waiting for transfers between devices: 4.15 us -> 2.29 us
    pallas_call x5, Pallas kernels: 18.9 us -> 13.2 us  [call(): pl.pallas_call(kernel, out_shape=out if isinstance(shape, list) else out[...]
    pallas_call x0 -> x2, Pallas kernels: none -> 4.24 us  [the longest x1 2.17 us: local(): pl.pallas_call(far_kernel, out_shape=half + parts, compiler_params=limits)]
    ppermute x1 -> x2, waiting for transfers between devices: 4.15 us -> 2.29 us  [the longest x1 2.28 us: local(): near_other = lax.ppermute(near_other, 'core', [(0, 1), (1, 0)])]
  transfers between devices with their start and end apart: 1 -> 2, of which waited for: 1 -> 1; matrix products, arithmetic and copies ran while one was open for 0% -> 0% of each run, Pallas kernels for 0% -> 1%
where the time goes in v4:
time: 171 us; the launch traced here: 170 us
  blocking collectives  147 us (86%)
  Pallas kernels  17.5 us (10%)
  local copies, waits for them, and re-layouts  2.55 us (1%)
  waiting for transfers between devices  2.29 us (1%)
    all_to_all x2, blocking collectives, local(): cells = lax.all_to_all(cells, DOMAIN, 0, 0, tiled=True)  78.3 us
    all_to_all x1, blocking collectives, local(): partial = lax.all_to_all(partial, CHIPS, 0, 0, tiled=True)  34.9 us
    all_to_all x1, blocking collectives, local(): lax.all_to_all(flat.reshape(BANDS, count, OB), BAND, 0, 0, tiled=True)  33.5 us
    pallas_call x5, Pallas kernels, call(): pl.pallas_call(kernel, out_shape=out if isinstance(shape, list) else out[...  13.2 us
  transfers between devices with their start and end apart: 2, of which 1 were waited for; matrix products, arithmetic and copies ran while one was open for 0% of the time, Pallas kernels for 1%

profile of v4, /device:TPU:0, one launch (start us, length us, event | category | flops | bytes accessed | tf_op | source)
XLA Modules:
  0.0 170.4 jit_solution(4470536698738388893)
XLA Ops:
  0.6 0.0 copy-start
  0.6 1.7 copy-done
  2.3 0.0 copy-start.2
  2.3 0.9 copy-done.2
  3.2 0.8 shard_map.50
  4.0 0.0 copy-start.1
  4.0 43.6 %all_to_all.20.cells = f32[16,328,128]{2,1,0:T(8,128)S(1)} all-to-all(f32[16,328,128]{2,1,0:T(8,128)S(1)} %shard_map.50), channel_id=1, replica_groups=mesh['x'=4,'y_lo'=2,'y_hi'=2,'z'=4,'core'=2] {'y_hi','z','core'}, dimensions={0} | all-to-all | bytes 5373952 | tf_op jit(solution)/shard_map/all_to_all | solution.py:239
  47.6 0.0 copy-done.1
  47.6 9.4 %shard_map.51 = f32[16,288,128]{2,1,0:T(8,128)S(1)} custom-call(f32[16,328,128]{2,1,0:T(8,128)S(1)} %all_to_all.20.cells, bf16[768,768]{1,0:T(8,128)(2,1)S(1)} %copy-done.1), custom_call_target="tpu_custom_call" | custom-call | tf_op jit(solution)/shard_map/pallas_call | solution.py:219
  57.0 34.6 %all_to_all.21.cells = f32[16,288,128]{2,1,0:T(8,128)S(1)} all-to-all(f32[16,288,128]{2,1,0:T(8,128)S(1)} %shard_map.51), channel_id=1, replica_groups=mesh['x'=4,'y_lo'=2,'y_hi'=2,'z'=4,'core'=2] {'y_hi','z','core'}, dimensions={0} | all-to-all | bytes 4718592 | tf_op jit(solution)/shard_map/all_to_all | solution.py:250
  91.7 2.1 %shard_map.52 = f32[4608,128]{1,0:T(8,128)} custom-call(f32[16,288,128]{2,1,0:T(8,128)S(1)} %all_to_all.21.cells), custom_call_target="tpu_custom_call" | custom-call | tf_op jit(solution)/shard_map/pallas_call | solution.py:219
  93.7 33.5 %all_to_all.22.cells = f32[8,576,128]{2,1,0:T(8,128)S(1)} all-to-all(f32[8,576,128]{2,1,0:T(8,128)} %bitcast.9), channel_id=1, replica_groups=mesh['x'=4,'y_lo'=2,'y_hi'=2,'z'=4,'core'=2] {'x','y_lo'}, dimensions={0} | all-to-all | bytes 4718592 | tf_op jit(solution)/shard_map/all_to_all | solution.py:253
  127.2 2.2 %shard_map.53 = (f32[2,4,4,64,128]{4,3,2,1,0:T(8,128)S(1)}, f32[2,4,4,64,128]{4,3,2,1,0:T(8,128)S(1)}, bf16[1024,576]{1,0:T(8,128)(2,1)S(1)}, bf16[1024,576]{1,0...) custom-call(f32[8,576,128]{2,1,0:T(8,128)S(1)} %all_to_all.22.cells), custom_call_target="tpu_custom_call" | custom-call | tf_op jit(solution)/shard_map/pallas_call | solution.py:259
  129.4 0.1 collective-permute-start
  129.5 2.1 %shard_map.54 = (f32[2,4,4,64,128]{4,3,2,1,0:T(8,128)S(1)}, f32[2,4,4,64,128]{4,3,2,1,0:T(8,128)S(1)}) custom-call(bf16[1024,576]{1,0:T(8,128)(2,1)S(1)} %get-tuple-element.12.left_hi, bf16[1024,576]{1,0:T(8,128)(2,1)S(1)} %get-tuple-element.13.left_lo, bf16[576,1024]{1,0:T(8,128)(2,1)S(1)} %get-tuple-element.14.right_hi, ...), custom_call_target="tpu_custom_call" | custom-call | tf_op jit(solution)/shard_map/pallas_call | solution.py:261
  131.6 0.6 collective-permute-start.1
  132.2 0.0 collective-permute-done.far_other
  132.2 2.3 %collective-permute-done.1.near_other = f32[2,4,4,64,128]{4,3,2,1,0:T(8,128)S(1)} collective-permute-done((f32[2,4,4,64,128]{4,3,2,1,0:T(8,128)S(1)}, f32[2,4,4,64,128]{4,3,2,1,0:T(8,128)S(1)}, u32[]{:S(2)}, u32[]{:S(2)}) %collective-permute-start.1) | collective-permute-done | bytes 1048608 | tf_op jit(solution)/shard_map/ppermute | solution.py:262
  134.4 0.2 shard_map.55
  134.7 34.9 %all_to_all.23.parts = f32[64,64,128]{2,1,0:T(8,128)S(1)} all-to-all(f32[64,64,128]{2,1,0:T(8,128)S(1)} %bitcast.6), channel_id=1, replica_groups=mesh['x'=4,'y_lo'=2,'y_hi'=2,'z'=4,'core'=2] {'x','y_lo','y_hi','z'}, dimensions={0} | all-to-all | bytes 4194304 | tf_op jit(solution)/shard_map/all_to_all | solution.py:265
  169.6 0.8 shard_map.56
Async XLA Ops:
  0.6 1.7 copy-start
  2.3 0.9 copy-start.2
  4.0 43.6 %copy-start.1 = (bf16[768,768]{1,0:T(8,128)(2,1)S(1)}, bf16[768,768]{1,0:T(8,128)(2,1)}, u32[]{:S(2)}) copy-start(bf16[768,768]{1,0:T(8,128)(2,1)} %constant.2.clone.ring) | copy-start | bytes 3538948
  129.4 2.7 %collective-permute-start = (f32[2,4,4,64,128]{4,3,2,1,0:T(8,128)S(1)}, f32[2,4,4,64,128]{4,3,2,1,0:T(8,128)S(1)}, u32[]{:S(2)}, u32[]{:S(2)}) collective-permute-start(f32[2,4,4,64,128]{4,3,2,1,0:T(8,128)S(1)} %get-tuple-element.11), channel_id=1, source_target_pairs={{0,1},{1,0},{2,3},{3,2},{4,5},{5,4},{6,7},{7,6},{8,9},{9,8},{10,11... | collective-permute-start | bytes 3145736 | tf_op jit(solution)/shard_map/ppermute | solution.py:260
  131.6 2.9 %collective-permute-start.1 = (f32[2,4,4,64,128]{4,3,2,1,0:T(8,128)S(1)}, f32[2,4,4,64,128]{4,3,2,1,0:T(8,128)S(1)}, u32[]{:S(2)}, u32[]{:S(2)}) collective-permute-start(f32[2,4,4,64,128]{4,3,2,1,0:T(8,128)S(1)} %get-tuple-element.17), channel_id=1, source_target_pairs={{0,1},{1,0},{2,3},{3,2},{4,5},{5,4},{6,7},{7,6},{8,9},{9,8},{10,11... | collective-permute-start | bytes 3145736 | tf_op jit(solution)/shard_map/ppermute | solution.py:262

commit v5 on v4

--- a/solution.py
+++ b/solution.py
@@ -186,12 +186,15 @@
             put(block.T, j, i)
 
 
-def far_kernel(cells, mine, others, left_hi, left_lo, right_hi, right_lo):
+def far_kernel(cells, flat, mine, others, left_hi, left_lo, right_hi, right_lo, result, done):
+    copy = pltpu.make_async_copy(flat, result, done)
+    copy.start()
     for b in range(BANDS):
         cols = slice(b * OB, (b + 1) * OB)
         right_hi[:, cols], right_lo[:, cols] = split(cells[b])
         left_hi[cols, :], left_lo[cols, :] = split(cells[b].T)
     margin_blocks((left_hi, left_lo, right_hi, right_lo), mine, others, [(2, 0), (3, 0), (2, 1), (3, 1)])
+    copy.wait()
 
 
 def near_kernel(left_hi, left_lo, right_hi, right_lo, mine, others):
@@ -256,7 +259,15 @@
     parts = (jax.ShapeDtypeStruct((NORB, count), jnp.bfloat16),) * 2
     parts += (jax.ShapeDtypeStruct((count, NORB), jnp.bfloat16),) * 2
     limits = pltpu.CompilerParams(vmem_limit_bytes=16 * MIB)
-    far, far_other, *parts = pl.pallas_call(far_kernel, out_shape=half + parts, compiler_params=limits)(points)
+    near_by, anywhere = pl.BlockSpec(memory_space=pltpu.VMEM), pl.BlockSpec(memory_space=pl.ANY)
+    far, far_other, *parts, result = pl.pallas_call(
+        far_kernel,
+        out_shape=half + parts + (jax.ShapeDtypeStruct(flat.shape, jnp.float32),),
+        in_specs=[near_by, anywhere],
+        out_specs=[near_by] * 6 + [anywhere],
+        scratch_shapes=[pltpu.SemaphoreType.DMA],
+        compiler_params=limits,
+    )(points, flat)
     far_other = lax.ppermute(far_other, "core", [(0, 1), (1, 0)])
     near, near_other = pl.pallas_call(near_kernel, out_shape=half, compiler_params=limits)(*parts)
     near_other = lax.ppermute(near_other, "core", [(0, 1), (1, 0)])
@@ -264,7 +275,7 @@
     partial = partial.reshape(BANDS * DOMS // 2, NORB // DOMS, OB)
     partial = lax.all_to_all(partial, CHIPS, 0, 0, tiled=True)
     margin = call(sum_kernel, (NORB // DOMS, OB), partial)
-    return flat.reshape(PL, NY, NZ, OB), margin.T
+    return result.reshape(PL, NY, NZ, OB), margin.T
 
 
 def solution(mesh):

time: 171 us -> 169 us (0.988)
  no operation moved by 1% of the time
where the time goes in v5:
time: 169 us
  blocking collectives  147 us (87%)
  Pallas kernels  16.1 us (10%)
  local copies, waits for them, and re-layouts  2.55 us (2%)
  waiting for transfers between devices  2.29 us (1%)
    all_to_all x2, blocking collectives, local(): cells = lax.all_to_all(cells, DOMAIN, 0, 0, tiled=True)  78.3 us
    all_to_all x1, blocking collectives, local(): partial = lax.all_to_all(partial, CHIPS, 0, 0, tiled=True)  34.9 us
    all_to_all x1, blocking collectives, local(): lax.all_to_all(flat.reshape(BANDS, count, OB), BAND, 0, 0, tiled=True)  33.3 us
    pallas_call x5, Pallas kernels, call(): pl.pallas_call(kernel, out_shape=out if isinstance(shape, list) else out[...  11.8 us
  transfers between devices with their start and end apart: 2, of which 1 were waited for; matrix products, arithmetic and copies ran while one was open for 0% of the time, Pallas kernels for 1%

profile of v5, /device:TPU:0, one launch (start us, length us, event | category | flops | bytes accessed | tf_op | source)
XLA Modules:
  0.0 168.8 jit_solution(17839991405182460163)
XLA Ops:
  0.6 0.0 copy-start
  0.6 1.7 copy-done
  2.3 0.0 copy-start.2
  2.3 0.9 copy-done.2
  3.2 0.8 shard_map.50
  4.0 0.0 copy-start.1
  4.0 43.6 %all_to_all.20.cells = f32[16,328,128]{2,1,0:T(8,128)S(1)} all-to-all(f32[16,328,128]{2,1,0:T(8,128)S(1)} %shard_map.50), channel_id=1, replica_groups=mesh['x'=4,'y_lo'=2,'y_hi'=2,'z'=4,'core'=2] {'y_hi','z','core'}, dimensions={0} | all-to-all | bytes 5373952 | tf_op jit(solution)/shard_map/all_to_all | solution.py:242
  47.6 0.0 copy-done.1
  47.6 9.4 %shard_map.51 = f32[16,288,128]{2,1,0:T(8,128)S(1)} custom-call(f32[16,328,128]{2,1,0:T(8,128)S(1)} %all_to_all.20.cells, bf16[768,768]{1,0:T(8,128)(2,1)S(1)} %copy-done.1), custom_call_target="tpu_custom_call" | custom-call | tf_op jit(solution)/shard_map/pallas_call | solution.py:222
  57.0 34.6 %all_to_all.21.cells = f32[16,288,128]{2,1,0:T(8,128)S(1)} all-to-all(f32[16,288,128]{2,1,0:T(8,128)S(1)} %shard_map.51), channel_id=1, replica_groups=mesh['x'=4,'y_lo'=2,'y_hi'=2,'z'=4,'core'=2] {'y_hi','z','core'}, dimensions={0} | all-to-all | bytes 4718592 | tf_op jit(solution)/shard_map/all_to_all | solution.py:253
  91.7 0.7 shard_map.52.flat
  92.3 33.3 %all_to_all.22.cells = f32[8,576,128]{2,1,0:T(8,128)S(1)} all-to-all(f32[8,576,128]{2,1,0:T(8,128)S(1)} %bitcast.6), channel_id=1, replica_groups=mesh['x'=4,'y_lo'=2,'y_hi'=2,'z'=4,'core'=2] {'x','y_lo'}, dimensions={0} | all-to-all | bytes 4718592 | tf_op jit(solution)/shard_map/all_to_all | solution.py:256
  125.6 2.2 %shard_map.53 = (f32[2,4,4,64,128]{4,3,2,1,0:T(8,128)S(1)}, f32[2,4,4,64,128]{4,3,2,1,0:T(8,128)S(1)}, bf16[1024,576]{1,0:T(8,128)(2,1)S(1)}, bf16[1024,576]{1,0...) custom-call(f32[8,576,128]{2,1,0:T(8,128)S(1)} %all_to_all.22.cells, ...), custom_call_target="tpu_custom_call" | custom-call | tf_op jit(solution)/shard_map/pallas_call | solution.py:263
  127.8 0.1 collective-permute-start
  127.9 2.1 %shard_map.54 = (f32[2,4,4,64,128]{4,3,2,1,0:T(8,128)S(1)}, f32[2,4,4,64,128]{4,3,2,1,0:T(8,128)S(1)}) custom-call(bf16[1024,576]{1,0:T(8,128)(2,1)S(1)} %get-tuple-element.14.left_hi, bf16[1024,576]{1,0:T(8,128)(2,1)S(1)} %get-tuple-element.15.left_lo, bf16[576,1024]{1,0:T(8,128)(2,1)S(1)} %get-tuple-element.16.right_hi, ...), custom_call_target="tpu_custom_call" | custom-call | tf_op jit(solution)/shard_map/pallas_call | solution.py:272
  130.0 0.6 collective-permute-start.1
  130.6 0.0 collective-permute-done.far_other
  130.6 2.3 %collective-permute-done.1.near_other = f32[2,4,4,64,128]{4,3,2,1,0:T(8,128)S(1)} collective-permute-done((f32[2,4,4,64,128]{4,3,2,1,0:T(8,128)S(1)}, f32[2,4,4,64,128]{4,3,2,1,0:T(8,128)S(1)}, u32[]{:S(2)}, u32[]{:S(2)}) %collective-permute-start.1) | collective-permute-done | bytes 1048608 | tf_op jit(solution)/shard_map/ppermute | solution.py:273
  132.8 0.2 shard_map.55
  133.1 34.9 %all_to_all.23.parts = f32[64,64,128]{2,1,0:T(8,128)S(1)} all-to-all(f32[64,64,128]{2,1,0:T(8,128)S(1)} %bitcast.7), channel_id=1, replica_groups=mesh['x'=4,'y_lo'=2,'y_hi'=2,'z'=4,'core'=2] {'x','y_lo','y_hi','z'}, dimensions={0} | all-to-all | bytes 4194304 | tf_op jit(solution)/shard_map/all_to_all | solution.py:276
  168.0 0.8 shard_map.56
Async XLA Ops:
  0.6 1.7 copy-start
  2.3 0.9 copy-start.2
  4.0 43.6 %copy-start.1 = (bf16[768,768]{1,0:T(8,128)(2,1)S(1)}, bf16[768,768]{1,0:T(8,128)(2,1)}, u32[]{:S(2)}) copy-start(bf16[768,768]{1,0:T(8,128)(2,1)} %constant.2.clone.ring) | copy-start | bytes 3538948
  127.8 2.7 %collective-permute-start = (f32[2,4,4,64,128]{4,3,2,1,0:T(8,128)S(1)}, f32[2,4,4,64,128]{4,3,2,1,0:T(8,128)S(1)}, u32[]{:S(2)}, u32[]{:S(2)}) collective-permute-start(f32[2,4,4,64,128]{4,3,2,1,0:T(8,128)S(1)} %get-tuple-element.13), channel_id=1, source_target_pairs={{0,1},{1,0},{2,3},{3,2},{4,5},{5,4},{6,7},{7,6},{8,9},{9,8},{10,11... | collective-permute-start | bytes 3145736 | tf_op jit(solution)/shard_map/ppermute | solution.py:271
  130.0 2.9 %collective-permute-start.1 = (f32[2,4,4,64,128]{4,3,2,1,0:T(8,128)S(1)}, f32[2,4,4,64,128]{4,3,2,1,0:T(8,128)S(1)}, u32[]{:S(2)}, u32[]{:S(2)}) collective-permute-start(f32[2,4,4,64,128]{4,3,2,1,0:T(8,128)S(1)} %get-tuple-element.19), channel_id=1, source_target_pairs={{0,1},{1,0},{2,3},{3,2},{4,5},{5,4},{6,7},{7,6},{8,9},{9,8},{10,11... | collective-permute-start | bytes 3145736 | tf_op jit(solution)/shard_map/ppermute | solution.py:273

commit v6 on v5

--- a/solution.py
+++ b/solution.py
@@ -67,7 +67,8 @@
                 m[i, (i - k) % n] += along[k]
         return m
 
-    return np.asarray(np.kron(ring(NY), np.eye(NZ)) + np.kron(np.eye(NY), ring(NZ)), jnp.bfloat16)
+    m = np.asarray(np.kron(ring(NY), np.eye(NZ)) + np.kron(np.eye(NY), ring(NZ)), jnp.bfloat16)
+    return np.concatenate([m, m], 0)
 
 
 def split(value):
@@ -75,12 +76,16 @@
     return hi, (value - hi.astype(jnp.float32)).astype(jnp.bfloat16)
 
 
-def spread_kernel(cells, pot, out):
+def spread_kernel(cells, out):
     for p in range(PL):
         flat = cells[p].T
         for j in range(LT):
             at = (p * LT + j) * OD
             out[:, at : at + OD, :] = flat[:, j * 128 : (j + 1) * 128].reshape(DOMS, OD, 128)
+
+
+def field_kernel(pot, cells, out, rows, done):
+    del cells
     turned = jnp.concatenate([(STRETCH * (pot[p] - center) + 3.0 * along[0]).T for p in range(PL)], 0)
     spot = lax.broadcasted_iota(jnp.int32, (NZ, PTS), 1)
     pick = (lax.rem(spot, NZ) == lax.broadcasted_iota(jnp.int32, (NZ, PTS), 0)).astype(jnp.float32)
@@ -91,9 +96,12 @@
     for p in range(PL):
         row = jnp.sum(jnp.where(keep, wide[p * NY : (p + 1) * NY, :], 0.0), 0, keepdims=True)
         for j in range(LT):
-            at = ROWS + p * LT + j
-            out[:, at : at + 1, :] = jnp.broadcast_to(row[None, :, j * 128 : (j + 1) * 128], (DOMS, 1, 128))
-    out[:, ROWS + POT :, :] = jnp.zeros((DOMS, POT_PAD - POT, 128), jnp.float32)
+            at = p * LT + j
+            rows[:, at : at + 1, :] = jnp.broadcast_to(row[None, :, j * 128 : (j + 1) * 128], (DOMS, 1, 128))
+    rows[:, POT:, :] = jnp.zeros((DOMS, POT_PAD - POT, 128), jnp.float32)
+    copy = pltpu.make_async_copy(rows, out.at[:, ROWS : ROWS + POT_PAD, :], done)
+    copy.start()
+    copy.wait()
 
 
 def filter_kernel(cells, ring, out, one, two, left_a, left_b, prod_a, prod_b):
@@ -110,10 +118,7 @@
         rows = slice(turn * group * PL * OD, (turn + 1) * group * PL * OD)
         for n in range(PTS // 256):
             cols = slice(n * 256, (n + 1) * 256)
-            prod[rows, cols] = (
-                jnp.dot(left[rows, :PTS], ring[:, cols], preferred_element_type=jnp.float32)
-                + jnp.dot(left[rows, PTS:], ring[:, cols], preferred_element_type=jnp.float32)
-            )
+            prod[rows, cols] = jnp.dot(left[rows, :], ring[:, cols], preferred_element_type=jnp.float32)
 
     def across(cur, prior, new, prod, left, back, scale, turn):
         for s in range(turn * group, (turn + 1) * group):
@@ -233,12 +238,21 @@
 
 
 def local(orbitals, potential, ring):
+    near_by, anywhere = pl.BlockSpec(memory_space=pltpu.VMEM), pl.BlockSpec(memory_space=pl.ANY)
     cells = call(
         spread_kernel,
         (DOMS, ROWS + POT_PAD, 128),
         orbitals.reshape(PL, PTS, OB),
-        potential.transpose(0, 2, 1),
     )
+    cells = pl.pallas_call(
+        field_kernel,
+        out_shape=jax.ShapeDtypeStruct(cells.shape, jnp.float32),
+        in_specs=[near_by, anywhere],
+        out_specs=anywhere,
+        scratch_shapes=[pltpu.VMEM((DOMS, POT_PAD, 128), jnp.float32), pltpu.SemaphoreType.DMA],
+        input_output_aliases={1: 0},
+        compiler_params=pltpu.CompilerParams(vmem_limit_bytes=16 * MIB),
+    )(potential.transpose(0, 2, 1), cells)
     cells = lax.all_to_all(cells, DOMAIN, 0, 0, tiled=True)
     cells = call(
         filter_kernel,
@@ -259,7 +273,6 @@
     parts = (jax.ShapeDtypeStruct((NORB, count), jnp.bfloat16),) * 2
     parts += (jax.ShapeDtypeStruct((count, NORB), jnp.bfloat16),) * 2
     limits = pltpu.CompilerParams(vmem_limit_bytes=16 * MIB)
-    near_by, anywhere = pl.BlockSpec(memory_space=pltpu.VMEM), pl.BlockSpec(memory_space=pl.ANY)
     far, far_other, *parts, result = pl.pallas_call(
         far_kernel,
         out_shape=half + parts + (jax.ShapeDtypeStruct(flat.shape, jnp.float32),),

time: 169 us -> 169 us (level)
  no operation moved by 1% of the time
where the time goes in v6:
time: 169 us
  blocking collectives  147 us (87%)
  Pallas kernels  16.5 us (10%)
  waiting for transfers between devices  2.29 us (1%)
  local copies, waits for them, and re-layouts  1.87 us (1%)
    all_to_all x2, blocking collectives, local(): cells = lax.all_to_all(cells, DOMAIN, 0, 0, tiled=True)  78.3 us
    all_to_all x1, blocking collectives, local(): partial = lax.all_to_all(partial, CHIPS, 0, 0, tiled=True)  34.9 us
    all_to_all x1, blocking collectives, local(): lax.all_to_all(flat.reshape(BANDS, count, OB), BAND, 0, 0, tiled=True)  33.3 us
    pallas_call x5, Pallas kernels, call(): pl.pallas_call(kernel, out_shape=out if isinstance(shape, list) else out[...  11.5 us
  transfers between devices with their start and end apart: 2, of which 1 were waited for; matrix products, arithmetic and copies ran while one was open for 0% of the time, Pallas kernels for 1%

profile of v6, /device:TPU:0, one launch (start us, length us, event | category | flops | bytes accessed | tf_op | source)
XLA Modules:
  0.0 168.6 jit_solution(1635983222266718254)
XLA Ops:
  0.6 0.0 copy-start.1
  0.6 1.7 copy-done.1
  2.3 0.0 copy-start.2
  2.3 0.7 shard_map.50.cells
  3.0 0.2 copy-done.2
  3.2 0.8 shard_map.51
  4.0 0.0 copy-start
  4.0 43.6 %all_to_all.20.cells = f32[16,328,128]{2,1,0:T(8,128)S(1)} all-to-all(f32[16,328,128]{2,1,0:T(8,128)S(1)} %shard_map.51), channel_id=1, replica_groups=mesh['x'=4,'y_lo'=2,'y_hi'=2,'z'=4,'core'=2] {'y_hi','z','core'}, dimensions={0} | all-to-all | bytes 5373952 | tf_op jit(solution)/shard_map/all_to_all | solution.py:256
  47.6 0.0 copy-done
  47.6 9.2 %shard_map.52 = f32[16,288,128]{2,1,0:T(8,128)S(1)} custom-call(f32[16,328,128]{2,1,0:T(8,128)S(1)} %all_to_all.20.cells, bf16[1536,768]{1,0:T(8,128)(2,1)S(1)} %copy-done), custom_call_target="tpu_custom_call" | custom-call | tf_op jit(solution)/shard_map/pallas_call | solution.py:227
  56.8 34.6 %all_to_all.21.cells = f32[16,288,128]{2,1,0:T(8,128)S(1)} all-to-all(f32[16,288,128]{2,1,0:T(8,128)S(1)} %shard_map.52), channel_id=1, replica_groups=mesh['x'=4,'y_lo'=2,'y_hi'=2,'z'=4,'core'=2] {'y_hi','z','core'}, dimensions={0} | all-to-all | bytes 4718592 | tf_op jit(solution)/shard_map/all_to_all | solution.py:267
  91.5 0.7 shard_map.53.flat
  92.1 33.3 %all_to_all.22.cells = f32[8,576,128]{2,1,0:T(8,128)S(1)} all-to-all(f32[8,576,128]{2,1,0:T(8,128)S(1)} %bitcast.6), channel_id=1, replica_groups=mesh['x'=4,'y_lo'=2,'y_hi'=2,'z'=4,'core'=2] {'x','y_lo'}, dimensions={0} | all-to-all | bytes 4718592 | tf_op jit(solution)/shard_map/all_to_all | solution.py:270
  125.4 2.2 %shard_map.54 = (f32[2,4,4,64,128]{4,3,2,1,0:T(8,128)S(1)}, f32[2,4,4,64,128]{4,3,2,1,0:T(8,128)S(1)}, bf16[1024,576]{1,0:T(8,128)(2,1)S(1)}, bf16[1024,576]{1,0...) custom-call(f32[8,576,128]{2,1,0:T(8,128)S(1)} %all_to_all.22.cells, ...), custom_call_target="tpu_custom_call" | custom-call | tf_op jit(solution)/shard_map/pallas_call | solution.py:276
  127.6 0.1 collective-permute-start
  127.7 2.1 %shard_map.55 = (f32[2,4,4,64,128]{4,3,2,1,0:T(8,128)S(1)}, f32[2,4,4,64,128]{4,3,2,1,0:T(8,128)S(1)}) custom-call(bf16[1024,576]{1,0:T(8,128)(2,1)S(1)} %get-tuple-element.14.left_hi, bf16[1024,576]{1,0:T(8,128)(2,1)S(1)} %get-tuple-element.15.left_lo, bf16[576,1024]{1,0:T(8,128)(2,1)S(1)} %get-tuple-element.16.right_hi, ...), custom_call_target="tpu_custom_call" | custom-call | tf_op jit(solution)/shard_map/pallas_call | solution.py:285
  129.8 0.6 collective-permute-start.1
  130.3 0.0 collective-permute-done.far_other
  130.3 2.3 %collective-permute-done.1.near_other = f32[2,4,4,64,128]{4,3,2,1,0:T(8,128)S(1)} collective-permute-done((f32[2,4,4,64,128]{4,3,2,1,0:T(8,128)S(1)}, f32[2,4,4,64,128]{4,3,2,1,0:T(8,128)S(1)}, u32[]{:S(2)}, u32[]{:S(2)}) %collective-permute-start.1) | collective-permute-done | bytes 1048608 | tf_op jit(solution)/shard_map/ppermute | solution.py:286
  132.6 0.2 shard_map.56
  132.8 34.9 %all_to_all.23.parts = f32[64,64,128]{2,1,0:T(8,128)S(1)} all-to-all(f32[64,64,128]{2,1,0:T(8,128)S(1)} %bitcast.7), channel_id=1, replica_groups=mesh['x'=4,'y_lo'=2,'y_hi'=2,'z'=4,'core'=2] {'x','y_lo','y_hi','z'}, dimensions={0} | all-to-all | bytes 4194304 | tf_op jit(solution)/shard_map/all_to_all | solution.py:289
  167.8 0.8 shard_map.57
Async XLA Ops:
  0.6 1.7 copy-start.1
  2.3 0.9 copy-start.2
  4.0 43.6 %copy-start = (bf16[1536,768]{1,0:T(8,128)(2,1)S(1)}, bf16[1536,768]{1,0:T(8,128)(2,1)}, u32[]{:S(2)}) copy-start(bf16[1536,768]{1,0:T(8,128)(2,1)} %constant.2.clone.ring) | copy-start | bytes 7077892
  127.6 2.7 %collective-permute-start = (f32[2,4,4,64,128]{4,3,2,1,0:T(8,128)S(1)}, f32[2,4,4,64,128]{4,3,2,1,0:T(8,128)S(1)}, u32[]{:S(2)}, u32[]{:S(2)}) collective-permute-start(f32[2,4,4,64,128]{4,3,2,1,0:T(8,128)S(1)} %get-tuple-element.13), channel_id=1, source_target_pairs={{0,1},{1,0},{2,3},{3,2},{4,5},{5,4},{6,7},{7,6},{8,9},{9,8},{10,11... | collective-permute-start | bytes 3145736 | tf_op jit(solution)/shard_map/ppermute | solution.py:284
  129.8 2.9 %collective-permute-start.1 = (f32[2,4,4,64,128]{4,3,2,1,0:T(8,128)S(1)}, f32[2,4,4,64,128]{4,3,2,1,0:T(8,128)S(1)}, u32[]{:S(2)}, u32[]{:S(2)}) collective-permute-start(f32[2,4,4,64,128]{4,3,2,1,0:T(8,128)S(1)} %get-tuple-element.19), channel_id=1, source_target_pairs={{0,1},{1,0},{2,3},{3,2},{4,5},{5,4},{6,7},{7,6},{8,9},{9,8},{10,11... | collective-permute-start | bytes 3145736 | tf_op jit(solution)/shard_map/ppermute | solution.py:286
